TPU v7x, 32 devices: a whole 2x2x4 slice. The times are simulated.
32 devices in a mesh: ctx: 16 (over z, x, core), tp: 2 (over y).
Axes of the slice: x: 2, y: 2, z: 4, core: 2. Of those that a mesh axis runs over, the one named last changes fastest.
Arguments:
- query: bfloat16 [2048, 4096], P(('ctx', 'tp')), may hold values from -200 to 200
- keys: bfloat16 [2048, 1024], P(('ctx', 'tp')), may hold values from -20 to 20
- values: bfloat16 [2048, 1024], P(('ctx', 'tp')), may hold values from -6 to 6
- output_gradient: bfloat16 [2048, 4096], P(('ctx', 'tp')), may hold values from -6 to 6
Outputs:
- attn_out: bfloat16 [2048, 4096], P(('ctx', 'tp'))
- grad_query: bfloat16 [2048, 4096], P(('ctx', 'tp'))
- key_gradient: bfloat16 [2048, 1024], P(('ctx', 'tp'))
- value_gradient: bfloat16 [2048, 1024], P(('ctx', 'tp'))
All inputs are finite; a program needn't handle non-finite values.
Results may differ from a plain program's by a relative error of at most 0.025.
Values may be sent and summed in bfloat16 or wider, within the bound.
A program may use at most 64 MiB of HBM per device.

v0:
```python
import jax
import jax.numpy as jnp
from jax import lax
from jax.sharding import PartitionSpec as P

HEAD_WIDTH = 128
QUERY_GROUP = 4


steps_per_turn = 4


def shifted(block, axis, distance):
    devices = range(lax.axis_size(axis))
    route = [((i - distance) % len(devices), i) for i in devices]
    return lax.ppermute(block, axis, route)


def shards(query, keys, values, output_gradient):
    ctx_count = lax.axis_size("ctx")
    ctx_index = lax.axis_index("ctx")
    queries_in, keys_in, values_in, grads_in = (
        lax.all_to_all(query, "tp", split_axis=1, concat_axis=0, tiled=True),
        lax.all_to_all(keys, "tp", split_axis=1, concat_axis=0, tiled=True),
        lax.all_to_all(values, "tp", split_axis=1, concat_axis=0, tiled=True),
        lax.all_to_all(output_gradient, "tp", split_axis=1, concat_axis=0, tiled=True),
    )
    tok_rows = queries_in.shape[0]
    kv_heads = keys_in.shape[1] // HEAD_WIDTH
    query_row_block = QUERY_GROUP * tok_rows
    score_scale = HEAD_WIDTH ** (-0.5)

    def to_rows(tensor):
        return (
            tensor.reshape(tok_rows, kv_heads, QUERY_GROUP, HEAD_WIDTH)
            .transpose(1, 2, 0, 3)
            .reshape(kv_heads, query_row_block, HEAD_WIDTH)
        )

    def from_rows(tensor):
        return (
            tensor.reshape(kv_heads, QUERY_GROUP, tok_rows, HEAD_WIDTH)
            .transpose(2, 0, 1, 3)
            .reshape(tok_rows, kv_heads * QUERY_GROUP * HEAD_WIDTH)
        )

    def from_keys(tensor):
        return tensor.transpose(1, 0, 2).reshape(tok_rows, kv_heads * HEAD_WIDTH)

    query_local = to_rows(queries_in)
    grad_local = to_rows(grads_in)
    whole_keys, whole_values = (
        lax.all_gather(keys_in, "ctx", axis=0, tiled=True),
        lax.all_gather(values_in, "ctx", axis=0, tiled=True),
    )
    key_major = whole_keys.reshape(-1, kv_heads, HEAD_WIDTH).transpose(1, 0, 2)
    value_major = whole_values.reshape(-1, kv_heads, HEAD_WIDTH).transpose(1, 0, 2)
    row_pos = ctx_index * tok_rows + jnp.arange(query_row_block) % tok_rows
    last_query = ctx_index * tok_rows + tok_rows - 1

    def masked_logits(first_key, key_count):
        key_block = lax.dynamic_slice_in_dim(key_major, first_key, key_count, 1)
        logits = score_scale * jnp.einsum(
            "hrd,hcd->hrc", query_local, key_block, preferred_element_type=jnp.float32
        )
        allowed = row_pos[:, None] >= first_key + jnp.arange(key_count, dtype=jnp.int32)[None, :]
        return (jnp.where(allowed[None], logits, -1e30), allowed)

    block_keys = steps_per_turn * tok_rows
    turn_count = ctx_count // steps_per_turn

    def stat_step(block_index, loop_state):
        first_key = block_index * block_keys

        def stat_update(old_state):
            running_max, running_sum = old_state
            logits, allowed = masked_logits(first_key, block_keys)
            new_max = jnp.maximum(running_max, jnp.max(logits, axis=2))
            terms = jnp.where(allowed[None], jnp.exp(logits - new_max[..., None]), 0.0)
            return (new_max, running_sum * jnp.exp(running_max - new_max) + jnp.sum(terms, axis=2))

        return lax.cond(
            first_key <= last_query, stat_update, lambda old_state: old_state, loop_state
        )

    start_max = jnp.full((kv_heads, query_row_block), -1e30, jnp.float32)
    start_sum = jnp.zeros((kv_heads, query_row_block), jnp.float32)
    running_max, running_sum = lax.fori_loop(0, turn_count, stat_step, (start_max, start_sum))
    lse = running_max + jnp.log(running_sum)

    def out_step(block_index, output_sum):
        first_key = block_index * block_keys

        def out_update(old_sum):
            logits, allowed = masked_logits(first_key, block_keys)
            weights = jnp.where(allowed[None], jnp.exp(logits - lse[..., None]), 0.0).astype(
                jnp.bfloat16
            )
            value_block = lax.dynamic_slice_in_dim(value_major, first_key, block_keys, 1)
            return old_sum + jnp.einsum(
                "hrc,hcd->hrd", weights, value_block, preferred_element_type=jnp.float32
            )

        return lax.cond(first_key <= last_query, out_update, lambda old_sum: old_sum, output_sum)

    output_sum = lax.fori_loop(
        0, turn_count, out_step, jnp.zeros((kv_heads, query_row_block, HEAD_WIDTH), jnp.float32)
    )
    attention = output_sum.astype(jnp.bfloat16)
    row_delta = jnp.sum(grad_local.astype(jnp.float32) * attention.astype(jnp.float32), axis=2)

    def gradients(first_key, key_count):
        logits, allowed = masked_logits(first_key, key_count)
        probs = jnp.where(allowed[None], jnp.exp(logits - lse[..., None]), 0.0)
        weights = probs.astype(jnp.bfloat16)
        key_block = lax.dynamic_slice_in_dim(key_major, first_key, key_count, 1)
        value_block = lax.dynamic_slice_in_dim(value_major, first_key, key_count, 1)
        value_part = jnp.einsum(
            "hrc,hrd->hcd", weights, grad_local, preferred_element_type=jnp.float32
        )
        prob_grad = jnp.einsum(
            "hrd,hcd->hrc", grad_local, value_block, preferred_element_type=jnp.float32
        )
        score_grad = (probs * (prob_grad - row_delta[..., None])).astype(jnp.bfloat16)
        query_part = jnp.einsum(
            "hrc,hcd->hrd", score_grad, key_block, preferred_element_type=jnp.float32
        )
        key_part = jnp.einsum(
            "hrc,hrd->hcd", score_grad, query_local, preferred_element_type=jnp.float32
        )
        return (query_part, jnp.stack([key_part, value_part]))

    def guarded(is_live, first_key, key_count):

        def nothing():
            return (
                jnp.zeros((kv_heads, query_row_block, HEAD_WIDTH), jnp.float32),
                jnp.zeros((2, kv_heads, key_count, HEAD_WIDTH), jnp.float32),
            )

        return lax.cond(is_live, lambda: gradients(first_key, key_count), nothing)

    start_query = jnp.zeros((kv_heads, query_row_block, HEAD_WIDTH), jnp.float32)

    def turn(turn_index, loop_state):
        query_sum, key_grads = loop_state
        for inner_step in range(steps_per_turn):
            cycle_step = turn_index * steps_per_turn + inner_step
            block_index = (ctx_index - cycle_step) % ctx_count
            query_part, pair_part = guarded(
                cycle_step <= ctx_index, block_index * tok_rows, tok_rows
            )
            query_sum = query_sum + query_part
            key_grads = shifted(key_grads + pair_part, "ctx", 1)
        return (query_sum, key_grads)

    start_pair = jnp.zeros((2, kv_heads, tok_rows, HEAD_WIDTH), jnp.float32)
    query_sum, key_grads = lax.fori_loop(0, turn_count, turn, (start_query, start_pair))
    grad_query = (score_scale * query_sum).astype(jnp.bfloat16)
    key_gradient = (score_scale * key_grads[0]).astype(jnp.bfloat16)
    value_gradient = key_grads[1].astype(jnp.bfloat16)
    return (
        lax.all_to_all(from_rows(attention), "tp", split_axis=0, concat_axis=1, tiled=True),
        lax.all_to_all(from_rows(grad_query), "tp", split_axis=0, concat_axis=1, tiled=True),
        lax.all_to_all(from_keys(key_gradient), "tp", split_axis=0, concat_axis=1, tiled=True),
        lax.all_to_all(from_keys(value_gradient), "tp", split_axis=0, concat_axis=1, tiled=True),
    )


def solution(mesh):
    placed = (
        P(("ctx", "tp"), None),
        P(("ctx", "tp"), None),
        P(("ctx", "tp"), None),
        P(("ctx", "tp"), None),
    )
    return jax.shard_map(
        shards,
        mesh=mesh,
        in_specs=placed,
        out_specs=(
            P(("ctx", "tp"), None),
            P(("ctx", "tp"), None),
            P(("ctx", "tp"), None),
            P(("ctx", "tp"), None),
        ),
        check_vma=False,
    )
```

profile of v0, /device:TPU:0, one launch (start us, length us, event | category | flops | bytes accessed | tf_op | source)
XLA Modules:
  0.0 390.5 jit_solution(13054810120384424918)
XLA Ops:
  8.2 8.6 %all_to_all.146 = bf16[64,2,512]{2,0,1:T(8,128)(2,1)} all-to-all(bf16[64,2,512]{2,0,1:T(8,128)(2,1)S(1)} %bitcast.213), channel_id=1, replica_groups=mesh['ctx'=16,'tp'=2] {'tp'}, dimensions={1} | all-to-all | bytes 262144 | tf_op jit(solution)/shard_map/all_to_all | solution.py:24
  17.8 7.5 %all_to_all.147 = bf16[64,2,512]{2,0,1:T(8,128)(2,1)} all-to-all(bf16[64,2,512]{2,0,1:T(8,128)(2,1)S(1)} %bitcast.214), channel_id=1, replica_groups=mesh['ctx'=16,'tp'=2] {'tp'}, dimensions={1} | all-to-all | bytes 262144 | tf_op jit(solution)/shard_map/all_to_all | solution.py:25
  27.2 3.5 all-to-all-start.1
  31.6 5.7 %all-to-all-done.1 = bf16[64,2,2048]{2,0,1:T(8,128)(2,1)S(1)} async-done(((bf16[64,2,2048]{2,0,1:T(8,128)(2,1)}), bf16[64,2,2048]{2,0,1:T(8,128)(2,1)S(1)}, u32[]{:S(2)}, u32[]{:S(2)}) %all-to-all-start.1) | async-done | bytes 524320 | tf_op jit(solution)/shard_map/all_to_all | solution.py:23
  37.3 3.5 all-to-all-start.4
  41.3 6.0 %all-to-all-done.4 = bf16[64,2,2048]{2,0,1:T(8,128)(2,1)S(1)} async-done(((bf16[64,2,2048]{2,0,1:T(8,128)(2,1)}), bf16[64,2,2048]{2,0,1:T(8,128)(2,1)S(1)}, u32[]{:S(2)}, u32[]{:S(2)}) %all-to-all-start.4) | async-done | bytes 524320 | tf_op jit(solution)/shard_map/all_to_all | solution.py:26
  47.9 11.1 %all-gather.3.cloned.1.call-done = bf16[2048,512]{1,0:T(8,128)(2,1)} async-done(((bf16[128,512]{1,0:T(8,128)(2,1)}), bf16[2048,512]{1,0:T(8,128)(2,1)}) %all-gather.3.cloned.1.call-update) | async-done | bytes 2097168 | tf_op jit(solution)/shard_map/all_gather | solution.py:53
  59.0 2.9 copy.61
  62.0 2.5 copy.67
  64.5 3.5 while.51
  64.5 3.3 conditional.18
  64.8 1.9 fusion.77
  68.0 33.4 %all-gather.5.cloned.1.call-done = bf16[2048,512]{1,0:T(8,128)(2,1)} async-done(((bf16[128,512]{1,0:T(8,128)(2,1)}), bf16[2048,512]{1,0:T(8,128)(2,1)}) %all-gather.5.cloned.1.call-update) | async-done | bytes 2097168 | tf_op jit(solution)/shard_map/all_gather | solution.py:54
  101.4 2.9 copy.66
  104.3 2.5 copy.68
  107.0 4.0 %while.52 = (s32[]{:T(128)}, f32[4,512,128]{2,1,0:T(8,128)S(1)}, s32[]{:T(128)}, bf16[4,2048,128]{2,1,0:T(8,128)(2,1)}, bf16[4,512,128]{2,1,0:T(8,128)(2,1)S(1)}...) while((s32[]{:T(128)}, f32[4,512,128]{2,1,0:T(8,128)S(1)}, ...), condition=%wide.region_9.10_spmd.clone, body=%wide.region_6.9_spmd.clone.sunk | while | flops 542642176 | bytes 4226333 | solution.py:106
  107.0 3.7 conditional.19
  107.3 3.5 fusion.87
  112.9 232.2 %while.53 = (s32[]{:T(128)}, f32[4,512,128]{2,1,0:T(8,128)}, f32[2,4,128,128]{3,2,1,0:T(8,128)}, s32[]{:T(128)}, bf16[4,2048,128]{2,1,0:T(8,128)(2,1)}, /*index=...) while((s32[]{:T(128)}, f32[4,512,128]{2,1,0:T(8,128)}, ...), condition=%wide.region_20.21_spmd.clone, body=%wide.region_11.20_spmd.clone.sunk | while | flops 1353191424 | bytes 60898796 | solution.py:158
  112.9 4.6 %conditional.23 = (f32[4,512,128]{2,1,0:T(8,128)S(1)}, f32[2,4,128,128]{3,2,1,0:T(8,128)S(1)}) conditional(s32[]{:T(128)} %convert_element_type.168, () %tuple.226, (s32[512]{0:T(512)S(1)}, s32[]{:T(128)}, s32[]{:T(128)}, bf16[4,2048,128]{2,1,0:T(8,128)(2,1)}, bf16[4,512,128]{2,1,0:T(8,128)(2,1)S(1)}, /*index=5*/f32[4,512]{1,0:T(4,128)S(1)}, ...), branch_computations={%region_12.12_spmd, %region_13.13_spmd} | conditional | flops 337838208 | bytes 9981127 | solution.py:141
  117.5 1.9 add.491
  120.6 19.2 %collective-permute-done = f32[2,4,128,128]{3,2,1,0:T(8,128)} collective-permute-done((f32[2,4,128,128]{3,2,1,0:T(8,128)}, f32[2,4,128,128]{3,2,1,0:T(8,128)}, u32[]{:S(2)}, u32[]{:S(2)}) %collective-permute-start) | collective-permute-done | bytes 524320 | tf_op jit(solution)/shard_map/while/body/eval_jaxpr/ppermute | solution.py:16
  139.8 2.1 add.492
  143.8 9.7 %collective-permute-done.1 = f32[2,4,128,128]{3,2,1,0:T(8,128)} collective-permute-done((f32[2,4,128,128]{3,2,1,0:T(8,128)}, f32[2,4,128,128]{3,2,1,0:T(8,128)}, u32[]{:S(2)}, u32[]{:S(2)}) %collective-permute-start.1) | collective-permute-done | bytes 524320 | tf_op jit(solution)/shard_map/while/body/eval_jaxpr/ppermute | solution.py:16
  153.5 2.1 add.493
  157.4 9.8 %collective-permute-done.2 = f32[2,4,128,128]{3,2,1,0:T(8,128)} collective-permute-done((f32[2,4,128,128]{3,2,1,0:T(8,128)}, f32[2,4,128,128]{3,2,1,0:T(8,128)}, u32[]{:S(2)}, u32[]{:S(2)}) %collective-permute-start.2) | collective-permute-done | bytes 524320 | tf_op jit(solution)/shard_map/while/body/eval_jaxpr/ppermute | solution.py:16
  167.2 2.0 add.494
  169.2 3.0 fusion.128
  172.3 8.6 %collective-permute-done.3 = f32[2,4,128,128]{3,2,1,0:T(8,128)} collective-permute-done((f32[2,4,128,128]{3,2,1,0:T(8,128)}, f32[2,4,128,128]{3,2,1,0:T(8,128)}, u32[]{:S(2)}, u32[]{:S(2)}) %collective-permute-start.3) | collective-permute-done | bytes 524320 | tf_op jit(solution)/shard_map/while/body/eval_jaxpr/ppermute | solution.py:16
  181.0 1.9 add.491
  183.8 10.7 %collective-permute-done = f32[2,4,128,128]{3,2,1,0:T(8,128)} collective-permute-done((f32[2,4,128,128]{3,2,1,0:T(8,128)}, f32[2,4,128,128]{3,2,1,0:T(8,128)}, u32[]{:S(2)}, u32[]{:S(2)}) %collective-permute-start) | collective-permute-done | bytes 524320 | tf_op jit(solution)/shard_map/while/body/eval_jaxpr/ppermute | solution.py:16
  194.6 2.1 add.492
  198.5 9.7 %collective-permute-done.1 = f32[2,4,128,128]{3,2,1,0:T(8,128)} collective-permute-done((f32[2,4,128,128]{3,2,1,0:T(8,128)}, f32[2,4,128,128]{3,2,1,0:T(8,128)}, u32[]{:S(2)}, u32[]{:S(2)}) %collective-permute-start.1) | collective-permute-done | bytes 524320 | tf_op jit(solution)/shard_map/while/body/eval_jaxpr/ppermute | solution.py:16
  208.2 2.1 add.493
  212.2 9.8 %collective-permute-done.2 = f32[2,4,128,128]{3,2,1,0:T(8,128)} collective-permute-done((f32[2,4,128,128]{3,2,1,0:T(8,128)}, f32[2,4,128,128]{3,2,1,0:T(8,128)}, u32[]{:S(2)}, u32[]{:S(2)}) %collective-permute-start.2) | collective-permute-done | bytes 524320 | tf_op jit(solution)/shard_map/while/body/eval_jaxpr/ppermute | solution.py:16
  221.9 2.0 add.494
  224.0 3.3 fusion.128
  227.3 8.3 %collective-permute-done.3 = f32[2,4,128,128]{3,2,1,0:T(8,128)} collective-permute-done((f32[2,4,128,128]{3,2,1,0:T(8,128)}, f32[2,4,128,128]{3,2,1,0:T(8,128)}, u32[]{:S(2)}, u32[]{:S(2)}) %collective-permute-start.3) | collective-permute-done | bytes 524320 | tf_op jit(solution)/shard_map/while/body/eval_jaxpr/ppermute | solution.py:16
  235.7 1.9 add.491
  238.6 10.7 %collective-permute-done = f32[2,4,128,128]{3,2,1,0:T(8,128)} collective-permute-done((f32[2,4,128,128]{3,2,1,0:T(8,128)}, f32[2,4,128,128]{3,2,1,0:T(8,128)}, u32[]{:S(2)}, u32[]{:S(2)}) %collective-permute-start) | collective-permute-done | bytes 524320 | tf_op jit(solution)/shard_map/while/body/eval_jaxpr/ppermute | solution.py:16
  249.3 2.1 add.492
  253.3 9.7 %collective-permute-done.1 = f32[2,4,128,128]{3,2,1,0:T(8,128)} collective-permute-done((f32[2,4,128,128]{3,2,1,0:T(8,128)}, f32[2,4,128,128]{3,2,1,0:T(8,128)}, u32[]{:S(2)}, u32[]{:S(2)}) %collective-permute-start.1) | collective-permute-done | bytes 524320 | tf_op jit(solution)/shard_map/while/body/eval_jaxpr/ppermute | solution.py:16
  263.0 2.1 add.493
  266.9 9.8 %collective-permute-done.2 = f32[2,4,128,128]{3,2,1,0:T(8,128)} collective-permute-done((f32[2,4,128,128]{3,2,1,0:T(8,128)}, f32[2,4,128,128]{3,2,1,0:T(8,128)}, u32[]{:S(2)}, u32[]{:S(2)}) %collective-permute-start.2) | collective-permute-done | bytes 524320 | tf_op jit(solution)/shard_map/while/body/eval_jaxpr/ppermute | solution.py:16
  276.7 2.0 add.494
  278.7 3.3 fusion.128
  282.1 8.3 %collective-permute-done.3 = f32[2,4,128,128]{3,2,1,0:T(8,128)} collective-permute-done((f32[2,4,128,128]{3,2,1,0:T(8,128)}, f32[2,4,128,128]{3,2,1,0:T(8,128)}, u32[]{:S(2)}, u32[]{:S(2)}) %collective-permute-start.3) | collective-permute-done | bytes 524320 | tf_op jit(solution)/shard_map/while/body/eval_jaxpr/ppermute | solution.py:16
  290.5 1.9 add.491
  293.3 10.7 %collective-permute-done = f32[2,4,128,128]{3,2,1,0:T(8,128)} collective-permute-done((f32[2,4,128,128]{3,2,1,0:T(8,128)}, f32[2,4,128,128]{3,2,1,0:T(8,128)}, u32[]{:S(2)}, u32[]{:S(2)}) %collective-permute-start) | collective-permute-done | bytes 524320 | tf_op jit(solution)/shard_map/while/body/eval_jaxpr/ppermute | solution.py:16
  304.0 2.1 add.492
  308.0 9.7 %collective-permute-done.1 = f32[2,4,128,128]{3,2,1,0:T(8,128)} collective-permute-done((f32[2,4,128,128]{3,2,1,0:T(8,128)}, f32[2,4,128,128]{3,2,1,0:T(8,128)}, u32[]{:S(2)}, u32[]{:S(2)}) %collective-permute-start.1) | collective-permute-done | bytes 524320 | tf_op jit(solution)/shard_map/while/body/eval_jaxpr/ppermute | solution.py:16
  317.7 2.1 add.493
  321.7 9.8 %collective-permute-done.2 = f32[2,4,128,128]{3,2,1,0:T(8,128)} collective-permute-done((f32[2,4,128,128]{3,2,1,0:T(8,128)}, f32[2,4,128,128]{3,2,1,0:T(8,128)}, u32[]{:S(2)}, u32[]{:S(2)}) %collective-permute-start.2) | collective-permute-done | bytes 524320 | tf_op jit(solution)/shard_map/while/body/eval_jaxpr/ppermute | solution.py:16
  331.4 2.0 add.494
  333.5 3.3 fusion.128
  336.8 8.3 %collective-permute-done.3 = f32[2,4,128,128]{3,2,1,0:T(8,128)} collective-permute-done((f32[2,4,128,128]{3,2,1,0:T(8,128)}, f32[2,4,128,128]{3,2,1,0:T(8,128)}, u32[]{:S(2)}, u32[]{:S(2)}) %collective-permute-start.3) | collective-permute-done | bytes 524320 | tf_op jit(solution)/shard_map/while/body/eval_jaxpr/ppermute | solution.py:16
  347.0 3.4 all-to-all-start.6
  352.2 2.7 all-to-all-done.6
  354.8 3.4 all-to-all-start.7
  360.0 2.7 all-to-all-done.7
  362.7 3.5 all-to-all-start.5
  367.8 5.0 %all-to-all-done.5 = bf16[2,64,2048]{2,1,0:T(8,128)(2,1)S(1)} async-done(((bf16[2,64,2048]{2,1,0:T(8,128)(2,1)}), bf16[2,64,2048]{2,1,0:T(8,128)(2,1)S(1)}, u32[]{:S(2)}, u32[]{:S(2)}) %all-to-all-start.5) | async-done | bytes 524320 | tf_op jit(solution)/shard_map/all_to_all | solution.py:164
  372.8 3.5 all-to-all-start.3
  378.4 4.4 %all-to-all-done.3 = bf16[2,64,2048]{2,1,0:T(8,128)(2,1)S(1)} async-done(((bf16[2,64,2048]{2,1,0:T(8,128)(2,1)}), bf16[2,64,2048]{2,1,0:T(8,128)(2,1)S(1)}, u32[]{:S(2)}, u32[]{:S(2)}) %all-to-all-start.3) | async-done | bytes 524320 | tf_op jit(solution)/shard_map/all_to_all | solution.py:163
  (143 shorter events, 62.4 us)
Async XLA Ops:
  7.2 23.6 %copy-start.2 = (bf16[64,4096]{1,0:T(8,128)(2,1)S(1)}, bf16[64,4096]{1,0:T(8,128)(2,1)}, u32[]{:S(2)}) copy-start(bf16[64,4096]{1,0:T(8,128)(2,1)} %param.25) | copy-start | bytes 1572868
  7.2 51.9 %all-gather.3.cloned.1.call-start = ((), (), s32[]{:S(2)}) async-start(), calls=%async_computation.8 | async-start | bytes 2228224 | tf_op jit(solution)/shard_map/all_gather | solution.py:53
  16.8 84.6 %all-gather.5.cloned.1.call-start = ((), (), s32[]{:S(2)}) async-start(), calls=%async_computation.9 | async-start | bytes 2228224 | tf_op jit(solution)/shard_map/all_gather | solution.py:54
  27.2 10.1 %all-to-all-start.1 = ((bf16[64,2,2048]{2,0,1:T(8,128)(2,1)}), bf16[64,2,2048]{2,0,1:T(8,128)(2,1)S(1)}, u32[]{:S(2)}, u32[]{:S(2)}) async-start(bf16[64,2,2048]{2,0,1:T(8,128)(2,1)} %bitcast.186), calls=%async_computation.1 | async-start | bytes 1048576 | tf_op jit(solution)/shard_map/all_to_all | solution.py:23
  37.3 10.1 %all-to-all-start.4 = ((bf16[64,2,2048]{2,0,1:T(8,128)(2,1)}), bf16[64,2,2048]{2,0,1:T(8,128)(2,1)S(1)}, u32[]{:S(2)}, u32[]{:S(2)}) async-start(bf16[64,2,2048]{2,0,1:T(8,128)(2,1)} %bitcast.185), calls=%async_computation.4 | async-start | bytes 1048576 | tf_op jit(solution)/shard_map/all_to_all | solution.py:26
  119.5 20.3 %collective-permute-start = (f32[2,4,128,128]{3,2,1,0:T(8,128)}, f32[2,4,128,128]{3,2,1,0:T(8,128)}, u32[]{:S(2)}, u32[]{:S(2)}) collective-permute-start(f32[2,4,128,128]{3,2,1,0:T(8,128)} %add.491), channel_id=1, source_target_pairs={{30,0},{0,2},{2,4},{4,6},{6,8},{8,10},{10,12},{12,14},{14,16},{16,... | collective-permute-start | bytes 1572872 | tf_op jit(solution)/shard_map/while/body/eval_jaxpr/ppermute | solution.py:16
  141.9 11.6 %collective-permute-start.1 = (f32[2,4,128,128]{3,2,1,0:T(8,128)}, f32[2,4,128,128]{3,2,1,0:T(8,128)}, u32[]{:S(2)}, u32[]{:S(2)}) collective-permute-start(f32[2,4,128,128]{3,2,1,0:T(8,128)} %add.492), channel_id=1, source_target_pairs={{30,0},{0,2},{2,4},{4,6},{6,8},{8,10},{10,12},{12,14},{14,16},{16,... | collective-permute-start | bytes 1572872 | tf_op jit(solution)/shard_map/while/body/eval_jaxpr/ppermute | solution.py:16
  155.6 11.6 %collective-permute-start.2 = (f32[2,4,128,128]{3,2,1,0:T(8,128)}, f32[2,4,128,128]{3,2,1,0:T(8,128)}, u32[]{:S(2)}, u32[]{:S(2)}) collective-permute-start(f32[2,4,128,128]{3,2,1,0:T(8,128)} %add.493), channel_id=1, source_target_pairs={{30,0},{0,2},{2,4},{4,6},{6,8},{8,10},{10,12},{12,14},{14,16},{16,... | collective-permute-start | bytes 1572872 | tf_op jit(solution)/shard_map/while/body/eval_jaxpr/ppermute | solution.py:16
  169.2 11.6 %collective-permute-start.3 = (f32[2,4,128,128]{3,2,1,0:T(8,128)}, f32[2,4,128,128]{3,2,1,0:T(8,128)}, u32[]{:S(2)}, u32[]{:S(2)}) collective-permute-start(f32[2,4,128,128]{3,2,1,0:T(8,128)} %add.494), channel_id=1, source_target_pairs={{30,0},{0,2},{2,4},{4,6},{6,8},{8,10},{10,12},{12,14},{14,16},{16,... | collective-permute-start | bytes 1572872 | tf_op jit(solution)/shard_map/while/body/eval_jaxpr/ppermute | solution.py:16
  182.9 11.6 %collective-permute-start = (f32[2,4,128,128]{3,2,1,0:T(8,128)}, f32[2,4,128,128]{3,2,1,0:T(8,128)}, u32[]{:S(2)}, u32[]{:S(2)}) collective-permute-start(f32[2,4,128,128]{3,2,1,0:T(8,128)} %add.491), channel_id=1, source_target_pairs={{30,0},{0,2},{2,4},{4,6},{6,8},{8,10},{10,12},{12,14},{14,16},{16,... | collective-permute-start | bytes 1572872 | tf_op jit(solution)/shard_map/while/body/eval_jaxpr/ppermute | solution.py:16
  196.6 11.6 %collective-permute-start.1 = (f32[2,4,128,128]{3,2,1,0:T(8,128)}, f32[2,4,128,128]{3,2,1,0:T(8,128)}, u32[]{:S(2)}, u32[]{:S(2)}) collective-permute-start(f32[2,4,128,128]{3,2,1,0:T(8,128)} %add.492), channel_id=1, source_target_pairs={{30,0},{0,2},{2,4},{4,6},{6,8},{8,10},{10,12},{12,14},{14,16},{16,... | collective-permute-start | bytes 1572872 | tf_op jit(solution)/shard_map/while/body/eval_jaxpr/ppermute | solution.py:16
  210.3 11.6 %collective-permute-start.2 = (f32[2,4,128,128]{3,2,1,0:T(8,128)}, f32[2,4,128,128]{3,2,1,0:T(8,128)}, u32[]{:S(2)}, u32[]{:S(2)}) collective-permute-start(f32[2,4,128,128]{3,2,1,0:T(8,128)} %add.493), channel_id=1, source_target_pairs={{30,0},{0,2},{2,4},{4,6},{6,8},{8,10},{10,12},{12,14},{14,16},{16,... | collective-permute-start | bytes 1572872 | tf_op jit(solution)/shard_map/while/body/eval_jaxpr/ppermute | solution.py:16
  224.0 11.6 %collective-permute-start.3 = (f32[2,4,128,128]{3,2,1,0:T(8,128)}, f32[2,4,128,128]{3,2,1,0:T(8,128)}, u32[]{:S(2)}, u32[]{:S(2)}) collective-permute-start(f32[2,4,128,128]{3,2,1,0:T(8,128)} %add.494), channel_id=1, source_target_pairs={{30,0},{0,2},{2,4},{4,6},{6,8},{8,10},{10,12},{12,14},{14,16},{16,... | collective-permute-start | bytes 1572872 | tf_op jit(solution)/shard_map/while/body/eval_jaxpr/ppermute | solution.py:16
  237.7 11.6 %collective-permute-start = (f32[2,4,128,128]{3,2,1,0:T(8,128)}, f32[2,4,128,128]{3,2,1,0:T(8,128)}, u32[]{:S(2)}, u32[]{:S(2)}) collective-permute-start(f32[2,4,128,128]{3,2,1,0:T(8,128)} %add.491), channel_id=1, source_target_pairs={{30,0},{0,2},{2,4},{4,6},{6,8},{8,10},{10,12},{12,14},{14,16},{16,... | collective-permute-start | bytes 1572872 | tf_op jit(solution)/shard_map/while/body/eval_jaxpr/ppermute | solution.py:16
  251.4 11.6 %collective-permute-start.1 = (f32[2,4,128,128]{3,2,1,0:T(8,128)}, f32[2,4,128,128]{3,2,1,0:T(8,128)}, u32[]{:S(2)}, u32[]{:S(2)}) collective-permute-start(f32[2,4,128,128]{3,2,1,0:T(8,128)} %add.492), channel_id=1, source_target_pairs={{30,0},{0,2},{2,4},{4,6},{6,8},{8,10},{10,12},{12,14},{14,16},{16,... | collective-permute-start | bytes 1572872 | tf_op jit(solution)/shard_map/while/body/eval_jaxpr/ppermute | solution.py:16
  265.1 11.6 %collective-permute-start.2 = (f32[2,4,128,128]{3,2,1,0:T(8,128)}, f32[2,4,128,128]{3,2,1,0:T(8,128)}, u32[]{:S(2)}, u32[]{:S(2)}) collective-permute-start(f32[2,4,128,128]{3,2,1,0:T(8,128)} %add.493), channel_id=1, source_target_pairs={{30,0},{0,2},{2,4},{4,6},{6,8},{8,10},{10,12},{12,14},{14,16},{16,... | collective-permute-start | bytes 1572872 | tf_op jit(solution)/shard_map/while/body/eval_jaxpr/ppermute | solution.py:16
  278.7 11.6 %collective-permute-start.3 = (f32[2,4,128,128]{3,2,1,0:T(8,128)}, f32[2,4,128,128]{3,2,1,0:T(8,128)}, u32[]{:S(2)}, u32[]{:S(2)}) collective-permute-start(f32[2,4,128,128]{3,2,1,0:T(8,128)} %add.494), channel_id=1, source_target_pairs={{30,0},{0,2},{2,4},{4,6},{6,8},{8,10},{10,12},{12,14},{14,16},{16,... | collective-permute-start | bytes 1572872 | tf_op jit(solution)/shard_map/while/body/eval_jaxpr/ppermute | solution.py:16
  292.4 11.6 %collective-permute-start = (f32[2,4,128,128]{3,2,1,0:T(8,128)}, f32[2,4,128,128]{3,2,1,0:T(8,128)}, u32[]{:S(2)}, u32[]{:S(2)}) collective-permute-start(f32[2,4,128,128]{3,2,1,0:T(8,128)} %add.491), channel_id=1, source_target_pairs={{30,0},{0,2},{2,4},{4,6},{6,8},{8,10},{10,12},{12,14},{14,16},{16,... | collective-permute-start | bytes 1572872 | tf_op jit(solution)/shard_map/while/body/eval_jaxpr/ppermute | solution.py:16
  306.1 11.6 %collective-permute-start.1 = (f32[2,4,128,128]{3,2,1,0:T(8,128)}, f32[2,4,128,128]{3,2,1,0:T(8,128)}, u32[]{:S(2)}, u32[]{:S(2)}) collective-permute-start(f32[2,4,128,128]{3,2,1,0:T(8,128)} %add.492), channel_id=1, source_target_pairs={{30,0},{0,2},{2,4},{4,6},{6,8},{8,10},{10,12},{12,14},{14,16},{16,... | collective-permute-start | bytes 1572872 | tf_op jit(solution)/shard_map/while/body/eval_jaxpr/ppermute | solution.py:16
  319.8 11.6 %collective-permute-start.2 = (f32[2,4,128,128]{3,2,1,0:T(8,128)}, f32[2,4,128,128]{3,2,1,0:T(8,128)}, u32[]{:S(2)}, u32[]{:S(2)}) collective-permute-start(f32[2,4,128,128]{3,2,1,0:T(8,128)} %add.493), channel_id=1, source_target_pairs={{30,0},{0,2},{2,4},{4,6},{6,8},{8,10},{10,12},{12,14},{14,16},{16,... | collective-permute-start | bytes 1572872 | tf_op jit(solution)/shard_map/while/body/eval_jaxpr/ppermute | solution.py:16
  333.5 11.6 %collective-permute-start.3 = (f32[2,4,128,128]{3,2,1,0:T(8,128)}, f32[2,4,128,128]{3,2,1,0:T(8,128)}, u32[]{:S(2)}, u32[]{:S(2)}) collective-permute-start(f32[2,4,128,128]{3,2,1,0:T(8,128)} %add.494), channel_id=1, source_target_pairs={{30,0},{0,2},{2,4},{4,6},{6,8},{8,10},{10,12},{12,14},{14,16},{16,... | collective-permute-start | bytes 1572872 | tf_op jit(solution)/shard_map/while/body/eval_jaxpr/ppermute | solution.py:16
  345.1 13.1 %copy-start = (f32[4,512,128]{2,1,0:T(8,128)S(1)}, f32[4,512,128]{2,1,0:T(8,128)}, u32[]{:S(2)}) copy-start(f32[4,512,128]{2,1,0:T(8,128)} %get-tuple-element.995) | copy-start | bytes 3145732
  347.0 7.8 %all-to-all-start.6 = ((bf16[2,64,512]{2,1,0:T(8,128)(2,1)}), bf16[2,64,512]{2,1,0:T(8,128)(2,1)S(1)}, u32[]{:S(2)}, u32[]{:S(2)}) async-start(bf16[2,64,512]{2,1,0:T(8,128)(2,1)} %all_to_all.130), calls=%async_computation.6 | async-start | bytes 262144 | tf_op jit(solution)/shard_map/all_to_all | solution.py:165
  354.8 7.8 %all-to-all-start.7 = ((bf16[2,64,512]{2,1,0:T(8,128)(2,1)}), bf16[2,64,512]{2,1,0:T(8,128)(2,1)S(1)}, u32[]{:S(2)}, u32[]{:S(2)}) async-start(bf16[2,64,512]{2,1,0:T(8,128)(2,1)} %all_to_all.134), calls=%async_computation.7 | async-start | bytes 262144 | tf_op jit(solution)/shard_map/all_to_all | solution.py:166
  358.2 7.9 %copy-start.1 = (bf16[4,512,128]{2,1,0:T(8,128)(2,1)S(1)}, bf16[4,512,128]{2,1,0:T(8,128)(2,1)}, u32[]{:S(2)}) copy-start(bf16[4,512,128]{2,1,0:T(8,128)(2,1)} %get-tuple-element.1291) | copy-start | bytes 1572868
  362.7 10.1 %all-to-all-start.5 = ((bf16[2,64,2048]{2,1,0:T(8,128)(2,1)}), bf16[2,64,2048]{2,1,0:T(8,128)(2,1)S(1)}, u32[]{:S(2)}, u32[]{:S(2)}) async-start(bf16[2,64,2048]{2,1,0:T(8,128)(2,1)} %all_to_all.126), calls=%async_computation.5 | async-start | bytes 1048576 | tf_op jit(solution)/shard_map/all_to_all | solution.py:164
  372.8 10.1 %all-to-all-start.3 = ((bf16[2,64,2048]{2,1,0:T(8,128)(2,1)}), bf16[2,64,2048]{2,1,0:T(8,128)(2,1)S(1)}, u32[]{:S(2)}, u32[]{:S(2)}) async-start(bf16[2,64,2048]{2,1,0:T(8,128)(2,1)} %all_to_all.119), calls=%async_computation.3 | async-start | bytes 1048576 | tf_op jit(solution)/shard_map/all_to_all | solution.py:163
Sparse Core Ops, SparseCore 0:
  16.9 42.0 all-gather.2
  61.2 40.1 all-gather.4
where the time goes:
time: 393 us; the launch traced here: 390 us
  waiting for transfers between devices  234 us (60%)
  other arithmetic  49.6 us (13%)
  local copies, waits for them, and re-layouts  45.3 us (12%)
  starting transfers between devices  21.1 us (5%)
  blocking collectives  16.1 us (4%)
  between operations  14.3 us (4%)
  matrix products  9.84 us (3%)
    ppermute x16, waiting for transfers between devices, shifted(): return lax.ppermute(block, axis, route)  163 us
    all_gather x1, waiting for transfers between devices, shards(): lax.all_gather(values_in, 'ctx', axis=0, tiled=True)  33.4 us
    add x16, other arithmetic, turn(): key_grads = shifted(key_grads + pair_part, 'ctx', 1)  32.6 us
    another operation x32, local copies, waits for them, and re-layouts  20 us
    add x4, other arithmetic, turn(): query_sum = query_sum + query_part  13 us
    all_gather x1, waiting for transfers between devices, shards(): lax.all_gather(keys_in, 'ctx', axis=0, tiled=True)  11.1 us
    all_to_all x1, blocking collectives, shards(): lax.all_to_all(keys, 'tp', split_axis=1, concat_axis=0, tiled=True)  8.61 us
  transfers between devices with their start and end apart: 24, of which 24 were waited for; matrix products, arithmetic and copies ran while one was open for 13% of the time, Pallas kernels for 0%

commit v1 on v0

v1 whole, which is shorter than its diff:
```python
import functools
import math

import jax
import jax.numpy as jnp
from jax import lax
from jax.experimental import pallas as pl
from jax.experimental.pallas import tpu as pltpu
from jax.sharding import PartitionSpec as P

HEAD_WIDTH = 128
MESH = pl.DeviceIdType.MESH
SCALE = HEAD_WIDTH ** (-0.5)
LOG2_SCALE = SCALE * math.log2(math.e)
MASKED = -1e30


def dot(a, b):
    return jnp.dot(a, b, preferred_element_type=jnp.float32)


def kernel(
    sizes,
    query, keys, values, grads,
    out_ref, dq_ref, dk_ref, dv_ref,
    q_all, g_all, kv_all, o_buf, dq_buf, fin,
    q_rows, q_cols, g_rows, g_cols, k_cols, v_cols,
    row_max, row_sum, lse, delta, acc, dq_acc, pair, part_out, part_in,
    own_sem, in_send, in_recv, kv_send, kv_recv, part_send, part_recv, out_send, out_recv,
):
    tp, inner, planes, tok, group, block = sizes
    peers = tp * inner
    chunk = peers * tok
    splits = chunk // block
    jobs = group * splits
    wide = group * HEAD_WIDTH
    ctx_index = lax.axis_index("ctx")
    tp_index = lax.axis_index("tp")
    plane = ctx_index // inner
    lane = ctx_index % inner
    me = lane * tp + tp_index

    def peer_id(p):
        return (plane * inner + p // tp, p % tp)

    def plane_id(z):
        return (z * inner + lane, tp_index)

    barrier = pltpu.get_barrier_semaphore()

    def greet(d, _):
        pl.semaphore_signal(
            barrier, inc=1, device_id=peer_id((me + d) % peers), device_id_type=MESH
        )
        return 0

    lax.fori_loop(1, peers, greet, 0)

    @pl.when(plane > 0)
    def _():
        pl.semaphore_signal(barrier, inc=1, device_id=plane_id(plane - 1), device_id_type=MESH)

    @pl.when(plane < planes - 1)
    def _():
        pl.semaphore_signal(barrier, inc=1, device_id=plane_id(plane + 1), device_id_type=MESH)

    expected = (
        (peers - 1)
        + jnp.where(plane > 0, 1, 0).astype(jnp.int32)
        + jnp.where(plane < planes - 1, 1, 0).astype(jnp.int32)
    )
    pl.semaphore_wait(barrier, expected)

    def cols(p, width):
        return pl.ds(pl.multiple_of(p * width, HEAD_WIDTH), width)

    def rows(p):
        return pl.ds(pl.multiple_of(p * tok, tok), tok)

    def in_pair(a, src_slot, dst_slot):
        if a == 0:
            return keys.at[:, cols(dst_slot, HEAD_WIDTH)], kv_all.at[plane, 0, rows(src_slot), :]
        if a == 1:
            return values.at[:, cols(dst_slot, HEAD_WIDTH)], kv_all.at[plane, 1, rows(src_slot), :]
        if a == 2:
            return query.at[:, cols(dst_slot, wide)], q_all.at[rows(src_slot), :]
        return grads.at[:, cols(dst_slot, wide)], g_all.at[rows(src_slot), :]

    def in_copy(a, src_slot, dst_slot):
        src, dst = in_pair(a, src_slot, dst_slot)
        return pltpu.make_async_remote_copy(
            src_ref=src, dst_ref=dst,
            send_sem=in_send.at[a, dst_slot], recv_sem=in_recv.at[a, src_slot],
            device_id=peer_id(dst_slot), device_id_type=MESH,
        )

    def own_copy(a):
        src, dst = in_pair(a, me, me)
        return pltpu.make_async_copy(src, dst, own_sem.at[a])

    def send_in(arrays):
        def one(d, _):
            for a in arrays:
                in_copy(a, me, (me + d) % peers).start()
            return 0

        lax.fori_loop(1, peers, one, 0)

    def await_in(arrays):
        for a in arrays:
            own_copy(a).wait()

        def one(d, _):
            for a in arrays:
                in_copy(a, (me + d) % peers, me).wait_recv()
            return 0

        lax.fori_loop(1, peers, one, 0)

    for a in range(4):
        own_copy(a).start()
    send_in((0, 1))
    send_in((2,))
    send_in((3,))

    def kv_copy(j, target):
        return pltpu.make_async_remote_copy(
            src_ref=kv_all.at[j], dst_ref=kv_all.at[j],
            send_sem=kv_send.at[j], recv_sem=kv_recv.at[j],
            device_id=plane_id(target), device_id_type=MESH,
        )

    await_in((0, 1))

    @pl.when(plane < planes - 1)
    def _():
        kv_copy(plane, plane + 1).start()

    def spread(whole, by_rows, by_cols):
        for h in range(group):
            for s in range(splits):
                piece = whole[s * block:(s + 1) * block, h * HEAD_WIDTH:(h + 1) * HEAD_WIDTH]
                by_rows[h * splits + s] = piece
                by_cols[h * splits + s] = piece.T

    await_in((2,))
    spread(q_all, q_rows, q_cols)

    key_pos = lax.broadcasted_iota(jnp.int32, (chunk, block), 0)
    query_pos = lax.broadcasted_iota(jnp.int32, (chunk, block), 1)

    def masked(i, s):
        return jnp.where(key_pos <= query_pos + (i % splits) * block, s, MASKED)

    v_cols[...] = kv_all[plane, 1].T

    def first(i, _):
        s = masked(i, dot(kv_all[plane, 0], q_cols[i]))
        top = jnp.max(s, axis=0, keepdims=True)
        p = jnp.exp2((s - top) * LOG2_SCALE)
        row_max[i] = top
        row_sum[i] = jnp.sum(p, axis=0, keepdims=True)
        acc[i] = dot(v_cols[...], p.astype(jnp.bfloat16))
        return 0

    lax.fori_loop(0, jobs, first, 0)

    def forward(n, _):
        j = plane - 1 - n
        kv_copy(j, plane).wait_recv()

        @pl.when(plane < planes - 1)
        def _():
            kv_copy(j, plane + 1).start()

        v_cols[...] = kv_all[j, 1].T

        def one(i, _):
            s = dot(kv_all[j, 0], q_cols[i])
            old = row_max[i]
            top = jnp.maximum(old, jnp.max(s, axis=0, keepdims=True))
            p = jnp.exp2((s - top) * LOG2_SCALE)
            shrink = jnp.exp2((old - top) * LOG2_SCALE)
            row_max[i] = top
            row_sum[i] = row_sum[i] * shrink + jnp.sum(p, axis=0, keepdims=True)
            acc[i] = acc[i] * shrink + dot(v_cols[...], p.astype(jnp.bfloat16))
            return 0

        lax.fori_loop(0, jobs, one, 0)
        return 0

    lax.fori_loop(0, plane, forward, 0)

    await_in((3,))
    spread(g_all, g_rows, g_cols)

    for h in range(group):
        for s in range(splits):
            i = h * splits + s
            total = row_sum[i]
            rounded = (acc[i] / total).astype(jnp.bfloat16)
            lse[i] = row_max[i] * LOG2_SCALE + jnp.log2(total)
            delta[i] = jnp.sum(
                g_cols[i].astype(jnp.float32) * rounded.astype(jnp.float32), axis=0, keepdims=True
            )
            o_buf[s * block:(s + 1) * block, h * HEAD_WIDTH:(h + 1) * HEAD_WIDTH] = rounded.T

    def out_pair(a, src_slot, dst_slot):
        if a == 0:
            return o_buf.at[rows(dst_slot), :], out_ref.at[:, cols(src_slot, wide)]
        if a == 1:
            return dq_buf.at[rows(dst_slot), :], dq_ref.at[:, cols(src_slot, wide)]
        if a == 2:
            return fin.at[0, rows(dst_slot), :], dk_ref.at[:, cols(src_slot, HEAD_WIDTH)]
        return fin.at[1, rows(dst_slot), :], dv_ref.at[:, cols(src_slot, HEAD_WIDTH)]

    def out_copy(a, src_slot, dst_slot):
        src, dst = out_pair(a, src_slot, dst_slot)
        return pltpu.make_async_remote_copy(
            src_ref=src, dst_ref=dst,
            send_sem=out_send.at[a, dst_slot], recv_sem=out_recv.at[a, src_slot],
            device_id=peer_id(dst_slot), device_id_type=MESH,
        )

    def own_out(a):
        src, dst = out_pair(a, me, me)
        return pltpu.make_async_copy(src, dst, own_sem.at[4 + a])

    def send_out(arrays):
        for a in arrays:
            own_out(a).start()

        def one(d, _):
            for a in arrays:
                out_copy(a, me, (me + d) % peers).start()
            return 0

        lax.fori_loop(1, peers, one, 0)

    send_out((0,))
    dq_acc[...] = jnp.zeros_like(dq_acc)

    def part_copy(j, target):
        return pltpu.make_async_remote_copy(
            src_ref=part_out.at[j], dst_ref=part_in.at[j],
            send_sem=part_send.at[j], recv_sem=part_recv.at[j],
            device_id=plane_id(target), device_id_type=MESH,
        )

    def backward(j, diagonal):
        pair[...] = jnp.zeros_like(pair)
        k_cols[...] = kv_all[j, 0].T

        def one(i, _):
            s = dot(kv_all[j, 0], q_cols[i])
            if diagonal:
                s = masked(i, s)
            p = jnp.exp2(s * LOG2_SCALE - lse[i])
            dp = dot(kv_all[j, 1], g_cols[i])
            ds = (p * (dp - delta[i])).astype(jnp.bfloat16)
            pair[1] += dot(p.astype(jnp.bfloat16), g_rows[i])
            pair[0] += dot(ds, q_rows[i])
            dq_acc[i] += dot(k_cols[...], ds)
            return 0

        lax.fori_loop(0, jobs, one, 0)

        @pl.when(plane < planes - 1)
        def _():
            part_copy(j, plane).wait_recv()
            pair[...] += part_in[j].astype(jnp.float32)

    def earlier(j, _):
        backward(j, False)
        part_out[j] = pair[...].astype(jnp.bfloat16)
        part_copy(j, plane - 1).start()
        return 0

    lax.fori_loop(0, plane, earlier, 0)
    backward(plane, True)
    fin[0] = (pair[0] * SCALE).astype(jnp.bfloat16)
    fin[1] = pair[1].astype(jnp.bfloat16)
    send_out((2, 3))
    for h in range(group):
        for s in range(splits):
            piece = (dq_acc[h * splits + s] * SCALE).astype(jnp.bfloat16)
            dq_buf[s * block:(s + 1) * block, h * HEAD_WIDTH:(h + 1) * HEAD_WIDTH] = piece.T
    send_out((1,))

    def drain(d, _):
        p = (me + d) % peers
        for a in range(4):
            in_copy(a, me, p).wait_send()
            out_copy(a, me, p).wait_send()
            out_copy(a, p, me).wait_recv()
        return 0

    lax.fori_loop(1, peers, drain, 0)
    for a in range(4):
        own_out(a).wait()

    @pl.when(plane < planes - 1)
    def _():
        def one(j, _):
            kv_copy(j, plane + 1).wait_send()
            return 0

        lax.fori_loop(0, plane + 1, one, 0)

    def sent(j, _):
        part_copy(j, plane - 1).wait_send()
        return 0

    lax.fori_loop(0, plane, sent, 0)


def shards(query, keys, values, output_gradient):
    ctx = lax.axis_size("ctx")
    tp = lax.axis_size("tp")
    tok, model = query.shape
    kv_heads = keys.shape[1] // HEAD_WIDTH
    group = model // keys.shape[1]
    inner = kv_heads // tp
    planes = ctx // inner
    peers = kv_heads
    chunk = peers * tok
    block = min(256, chunk)
    jobs = group * (chunk // block)
    wide = group * HEAD_WIDTH
    bf16, f32 = jnp.bfloat16, jnp.float32
    hbm = pl.BlockSpec(memory_space=pl.ANY)
    dma = pltpu.SemaphoreType.DMA
    return pl.pallas_call(
        functools.partial(kernel, (tp, inner, planes, tok, group, block)),
        out_shape=tuple(
            jax.ShapeDtypeStruct(a.shape, a.dtype) for a in (query, query, keys, values)
        ),
        in_specs=[hbm] * 4,
        out_specs=(hbm,) * 4,
        scratch_shapes=[
            pltpu.VMEM((chunk, wide), bf16),
            pltpu.VMEM((chunk, wide), bf16),
            pltpu.VMEM((planes, 2, chunk, HEAD_WIDTH), bf16),
            pltpu.VMEM((chunk, wide), bf16),
            pltpu.VMEM((chunk, wide), bf16),
            pltpu.VMEM((2, chunk, HEAD_WIDTH), bf16),
            pltpu.VMEM((jobs, block, HEAD_WIDTH), bf16),
            pltpu.VMEM((jobs, HEAD_WIDTH, block), bf16),
            pltpu.VMEM((jobs, block, HEAD_WIDTH), bf16),
            pltpu.VMEM((jobs, HEAD_WIDTH, block), bf16),
            pltpu.VMEM((HEAD_WIDTH, chunk), bf16),
            pltpu.VMEM((HEAD_WIDTH, chunk), bf16),
            pltpu.VMEM((jobs, 1, block), f32),
            pltpu.VMEM((jobs, 1, block), f32),
            pltpu.VMEM((jobs, 1, block), f32),
            pltpu.VMEM((jobs, 1, block), f32),
            pltpu.VMEM((jobs, HEAD_WIDTH, block), f32),
            pltpu.VMEM((jobs, HEAD_WIDTH, block), f32),
            pltpu.VMEM((2, chunk, HEAD_WIDTH), f32),
            pltpu.VMEM((planes, 2, chunk, HEAD_WIDTH), bf16),
            pltpu.VMEM((planes, 2, chunk, HEAD_WIDTH), bf16),
            dma((8,)),
            dma((4, peers)),
            dma((4, peers)),
            dma((planes,)),
            dma((planes,)),
            dma((planes,)),
            dma((planes,)),
            dma((4, peers)),
            dma((4, peers)),
        ],
        compiler_params=pltpu.CompilerParams(
            collective_id=0, has_side_effects=True, vmem_limit_bytes=48 * 1024 * 1024
        ),
    )(query, keys, values, output_gradient)


def solution(mesh):
    placed = (P(("ctx", "tp"), None),) * 4
    return jax.shard_map(
        shards, mesh=mesh, in_specs=placed, out_specs=placed, check_vma=False
    )
```

time: 393 us -> 82 us (0.21)
  waiting for transfers between devices: 234 us -> 0 us
  Pallas kernels: 0 us -> 74.3 us
  other arithmetic: 49.6 us -> 0 us
  local copies, waits for them, and re-layouts: 45.3 us -> 6.78 us
  starting transfers between devices: 21.1 us -> 0 us
  blocking collectives: 16.1 us -> 0 us
  between operations: 14.3 us -> 0.65 us
  matrix products: 9.84 us -> 0 us
    ppermute x16 -> x0, waiting for transfers between devices: 163 us -> none  [shifted(): return lax.ppermute(block, axis, route)]
    pallas_call x0 -> x1, Pallas kernels: none -> 74.3 us  [shards(): pl.pallas_call(functools.partial(kernel, (tp, inner, planes, tok, group,...]
    add x29 -> x0, other arithmetic: 45.7 us -> none  [the longest x16 32.6 us: turn(): key_grads = shifted(key_grads + pair_part, 'ctx', 1)]
    all_gather x2 -> x0, waiting for transfers between devices: 44.5 us -> none  [the longest x1 33.4 us: shards(): lax.all_gather(values_in, 'ctx', axis=0, tiled=True)]
    all_to_all x6 -> x0, waiting for transfers between devices: 26.5 us -> none  [the longest x1 6.03 us: shards(): lax.all_to_all(output_gradient, 'tp', split_axis=1, concat_axis=0, tiled=...]
    all_to_all x6 -> x0, starting transfers between devices: 20.7 us -> none  [the longest x1 3.49 us: shards(): lax.all_to_all(query, 'tp', split_axis=1, concat_axis=0, tiled=True)]
    another operation x40 -> x0, local copies, waits for them, and re-layouts: 20 us -> none
    all_to_all x2 -> x0, blocking collectives: 16.1 us -> none  [the longest x1 8.61 us: shards(): lax.all_to_all(keys, 'tp', split_axis=1, concat_axis=0, tiled=True)]
  transfers between devices with their start and end apart: 24 -> 0, of which waited for: 24 -> 0; matrix products, arithmetic and copies ran while one was open for 13% -> 0% of each run, Pallas kernels for 0% -> 0%
where the time goes in v1:
time: 82 us; the launch traced here: 81.7 us
  Pallas kernels  74.3 us (91%)
  local copies, waits for them, and re-layouts  6.78 us (8%)
    pallas_call x1, Pallas kernels, shards(): pl.pallas_call(functools.partial(kernel, (tp, inner, planes, tok, group,...  74.3 us
    unnamed x12, local copies, waits for them, and re-layouts  6.78 us

profile of v1, /device:TPU:0, one launch (start us, length us, event | category | flops | bytes accessed | tf_op | source)
XLA Modules:
  0.0 81.7 jit_solution(1294531437479991956)
XLA Ops:
  0.6 0.0 copy-start
  0.6 1.0 %copy-done = bf16[64,4096]{1,0:T(8,128)(2,1)S(1)} copy-done((bf16[64,4096]{1,0:T(8,128)(2,1)S(1)}, bf16[64,4096]{1,0:T(8,128)(2,1)}, u32[]{:S(2)}) %copy-start) | copy-done | bytes 524312
  1.7 0.0 copy-start.1
  1.7 1.0 %copy-done.1 = bf16[64,4096]{1,0:T(8,128)(2,1)S(1)} copy-done((bf16[64,4096]{1,0:T(8,128)(2,1)S(1)}, bf16[64,4096]{1,0:T(8,128)(2,1)}, u32[]{:S(2)}) %copy-start.1) | copy-done | bytes 524312
  2.7 0.0 copy-start.2
  2.7 0.9 %copy-done.2 = bf16[64,1024]{1,0:T(8,128)(2,1)S(1)} copy-done((bf16[64,1024]{1,0:T(8,128)(2,1)S(1)}, bf16[64,1024]{1,0:T(8,128)(2,1)}, u32[]{:S(2)}) %copy-start.2) | copy-done | bytes 131096
  3.6 0.0 copy-start.3
  3.6 0.9 %copy-done.3 = bf16[64,1024]{1,0:T(8,128)(2,1)S(1)} copy-done((bf16[64,1024]{1,0:T(8,128)(2,1)S(1)}, bf16[64,1024]{1,0:T(8,128)(2,1)}, u32[]{:S(2)}) %copy-start.3) | copy-done | bytes 131096
  4.5 74.3 %shard_map.75 = (bf16[64,4096]{1,0:T(8,128)(2,1)S(1)}, bf16[64,4096]{1,0:T(8,128)(2,1)S(1)}, bf16[64,1024]{1,0:T(8,128)(2,1)S(1)}, bf16[64,1024]{1,0:T(8,128)(2,1)S(1)}) custom-call(bf16[64,4096]{1,0:T(8,128)(2,1)S(1)} %copy-done, bf16[64,1024]{1,0:T(8,128)(2,1)S(1)} %copy-done.2, bf16[64,1024]{1,0:T(8,128)(2,1)S(1)} %copy-done.3, bf16[64,4096]{1,0:T(8,128)(2,1)S(1)} %copy-done.1), custom_call_target="tpu_custom_call" | custom-call | tf_op jit(solution)/shard_map/pallas_call | solution.py:333
  78.8 0.8 copy.12
  79.6 0.8 copy.13
  80.4 0.7 copy.14
  81.1 0.7 copy.15
Async XLA Ops:
  0.6 1.0 %copy-start = (bf16[64,4096]{1,0:T(8,128)(2,1)S(1)}, bf16[64,4096]{1,0:T(8,128)(2,1)}, u32[]{:S(2)}) copy-start(bf16[64,4096]{1,0:T(8,128)(2,1)} %query.1) | copy-start | bytes 1572868
  1.7 1.0 %copy-start.1 = (bf16[64,4096]{1,0:T(8,128)(2,1)S(1)}, bf16[64,4096]{1,0:T(8,128)(2,1)}, u32[]{:S(2)}) copy-start(bf16[64,4096]{1,0:T(8,128)(2,1)} %grads.1) | copy-start | bytes 1572868
  2.7 0.9 %copy-start.2 = (bf16[64,1024]{1,0:T(8,128)(2,1)S(1)}, bf16[64,1024]{1,0:T(8,128)(2,1)}, u32[]{:S(2)}) copy-start(bf16[64,1024]{1,0:T(8,128)(2,1)} %keys.1) | copy-start | bytes 393220
  3.6 0.9 %copy-start.3 = (bf16[64,1024]{1,0:T(8,128)(2,1)S(1)}, bf16[64,1024]{1,0:T(8,128)(2,1)}, u32[]{:S(2)}) copy-start(bf16[64,1024]{1,0:T(8,128)(2,1)} %values.1) | copy-start | bytes 393220

commit v2 on v1

--- a/solution.py
+++ b/solution.py
@@ -25,7 +25,7 @@
     out_ref, dq_ref, dk_ref, dv_ref,
     q_all, g_all, kv_all, o_buf, dq_buf, fin,
     q_rows, q_cols, g_rows, g_cols, k_cols, v_cols,
-    row_max, row_sum, lse, delta, acc, dq_acc, pair, part_out, part_in,
+    row_max, row_sum, lse, delta, acc, o_cols, dq_acc, pair, part_out, part_in,
     own_sem, in_send, in_recv, kv_send, kv_recv, part_send, part_recv, out_send, out_recv,
 ):
     tp, inner, planes, tok, group, block = sizes
@@ -131,10 +131,19 @@
         )
 
     await_in((0, 1))
+    top_plane = plane == planes - 1
 
     @pl.when(plane < planes - 1)
     def _():
         kv_copy(plane, plane + 1).start()
+
+        def relay(n, _):
+            j = plane - 1 - n
+            kv_copy(j, plane).wait_recv()
+            kv_copy(j, plane + 1).start()
+            return 0
+
+        lax.fori_loop(0, plane, relay, 0)
 
     def spread(whole, by_rows, by_cols):
         for h in range(group):
@@ -146,32 +155,45 @@
     await_in((2,))
     spread(q_all, q_rows, q_cols)
 
-    key_pos = lax.broadcasted_iota(jnp.int32, (chunk, block), 0)
-    query_pos = lax.broadcasted_iota(jnp.int32, (chunk, block), 1)
-
-    def masked(i, s):
-        return jnp.where(key_pos <= query_pos + (i % splits) * block, s, MASKED)
+    def masked(s, split):
+        shape = s.shape
+        key_pos = lax.broadcasted_iota(jnp.int32, shape, 0)
+        query_pos = lax.broadcasted_iota(jnp.int32, shape, 1) + split * block
+        return jnp.where(key_pos <= query_pos, s, MASKED)
 
     v_cols[...] = kv_all[plane, 1].T
 
-    def first(i, _):
-        s = masked(i, dot(kv_all[plane, 0], q_cols[i]))
-        top = jnp.max(s, axis=0, keepdims=True)
-        p = jnp.exp2((s - top) * LOG2_SCALE)
-        row_max[i] = top
-        row_sum[i] = jnp.sum(p, axis=0, keepdims=True)
-        acc[i] = dot(v_cols[...], p.astype(jnp.bfloat16))
-        return 0
-
-    lax.fori_loop(0, jobs, first, 0)
+    def first(h, _):
+        for split in range(splits):
+            i, seen = h * splits + split, (split + 1) * block
+            s = masked(dot(kv_all[plane, 0, :seen], q_cols[i]), split)
+            top = jnp.max(s, axis=0, keepdims=True)
+            p = jnp.exp2((s - top) * LOG2_SCALE)
+            row_max[i] = top
+            row_sum[i] = jnp.sum(p, axis=0, keepdims=True)
+            acc[i] = dot(v_cols[:, :seen], p.astype(jnp.bfloat16))
+        return 0
+
+    lax.fori_loop(0, group, first, 0)
+
+    def take_grads():
+        await_in((3,))
+        spread(g_all, g_rows, g_cols)
+
+    @pl.when(plane == 0)
+    def _():
+        take_grads()
 
     def forward(n, _):
         j = plane - 1 - n
-        kv_copy(j, plane).wait_recv()
-
-        @pl.when(plane < planes - 1)
+
+        @pl.when(j == 0)
         def _():
-            kv_copy(j, plane + 1).start()
+            take_grads()
+
+        @pl.when(top_plane)
+        def _():
+            kv_copy(j, plane).wait_recv()
 
         v_cols[...] = kv_all[j, 1].T
 
@@ -191,19 +213,14 @@
 
     lax.fori_loop(0, plane, forward, 0)
 
-    await_in((3,))
-    spread(g_all, g_rows, g_cols)
-
-    for h in range(group):
-        for s in range(splits):
-            i = h * splits + s
-            total = row_sum[i]
-            rounded = (acc[i] / total).astype(jnp.bfloat16)
-            lse[i] = row_max[i] * LOG2_SCALE + jnp.log2(total)
-            delta[i] = jnp.sum(
-                g_cols[i].astype(jnp.float32) * rounded.astype(jnp.float32), axis=0, keepdims=True
-            )
-            o_buf[s * block:(s + 1) * block, h * HEAD_WIDTH:(h + 1) * HEAD_WIDTH] = rounded.T
+    for i in range(jobs):
+        total = row_sum[i]
+        rounded = (acc[i] / total).astype(jnp.bfloat16)
+        o_cols[i] = rounded
+        lse[i] = row_max[i] * LOG2_SCALE + jnp.log2(total)
+        delta[i] = jnp.sum(
+            g_cols[i].astype(jnp.float32) * rounded.astype(jnp.float32), axis=0, keepdims=True
+        )
 
     def out_pair(a, src_slot, dst_slot):
         if a == 0:
@@ -237,7 +254,6 @@
 
         lax.fori_loop(1, peers, one, 0)
 
-    send_out((0,))
     dq_acc[...] = jnp.zeros_like(dq_acc)
 
     def part_copy(j, target):
@@ -247,45 +263,76 @@
             device_id=plane_id(target), device_id_type=MESH,
         )
 
+    def gradients(j, i, seen, split):
+        s = dot(kv_all[j, 0, :seen], q_cols[i])
+        if split is not None:
+            s = masked(s, split)
+        p = jnp.exp2(s * LOG2_SCALE - lse[i])
+        dp = dot(kv_all[j, 1, :seen], g_cols[i])
+        ds = (p * (dp - delta[i])).astype(jnp.bfloat16)
+        pair[j, 1, :seen] += dot(p.astype(jnp.bfloat16), g_rows[i])
+        pair[j, 0, :seen] += dot(ds, q_rows[i])
+        dq_acc[i] += dot(k_cols[:, :seen], ds)
+
     def backward(j, diagonal):
-        pair[...] = jnp.zeros_like(pair)
+        pair[j] = jnp.zeros(pair.shape[1:], jnp.float32)
         k_cols[...] = kv_all[j, 0].T
 
         def one(i, _):
-            s = dot(kv_all[j, 0], q_cols[i])
-            if diagonal:
-                s = masked(i, s)
-            p = jnp.exp2(s * LOG2_SCALE - lse[i])
-            dp = dot(kv_all[j, 1], g_cols[i])
-            ds = (p * (dp - delta[i])).astype(jnp.bfloat16)
-            pair[1] += dot(p.astype(jnp.bfloat16), g_rows[i])
-            pair[0] += dot(ds, q_rows[i])
-            dq_acc[i] += dot(k_cols[...], ds)
-            return 0
-
-        lax.fori_loop(0, jobs, one, 0)
-
-        @pl.when(plane < planes - 1)
-        def _():
-            part_copy(j, plane).wait_recv()
-            pair[...] += part_in[j].astype(jnp.float32)
+            gradients(j, i, chunk, None)
+            return 0
+
+        def triangle(h, _):
+            for split in range(splits):
+                gradients(j, h * splits + split, (split + 1) * block, split)
+            return 0
+
+        if diagonal:
+            lax.fori_loop(0, group, triangle, 0)
+        else:
+            lax.fori_loop(0, jobs, one, 0)
 
     def earlier(j, _):
         backward(j, False)
-        part_out[j] = pair[...].astype(jnp.bfloat16)
-        part_copy(j, plane - 1).start()
+
+        @pl.when(top_plane)
+        def _():
+            part_out[j] = pair[j].astype(jnp.bfloat16)
+            part_copy(j, plane - 1).start()
+
         return 0
 
     lax.fori_loop(0, plane, earlier, 0)
+
+    def gather_cols(pieces, dst, factor):
+        for h in range(group):
+            for s in range(splits):
+                piece = pieces[h * splits + s]
+                if factor is not None:
+                    piece = (piece * factor).astype(jnp.bfloat16)
+                dst[s * block:(s + 1) * block, h * HEAD_WIDTH:(h + 1) * HEAD_WIDTH] = piece.T
+
+    gather_cols(o_cols, o_buf, None)
+    send_out((0,))
     backward(plane, True)
-    fin[0] = (pair[0] * SCALE).astype(jnp.bfloat16)
-    fin[1] = pair[1].astype(jnp.bfloat16)
+    gather_cols(dq_acc, dq_buf, SCALE)
+    send_out((1,))
+
+    @pl.when(plane < planes - 1)
+    def _():
+        def chain(j, _):
+            part_copy(j, plane).wait_recv()
+            part_out[j] = (pair[j] + part_in[j].astype(jnp.float32)).astype(jnp.bfloat16)
+            part_copy(j, plane - 1).start()
+            return 0
+
+        lax.fori_loop(0, plane, chain, 0)
+        part_copy(plane, plane).wait_recv()
+        pair[plane] += part_in[plane].astype(jnp.float32)
+
+    fin[0] = (pair[plane, 0] * SCALE).astype(jnp.bfloat16)
+    fin[1] = pair[plane, 1].astype(jnp.bfloat16)
     send_out((2, 3))
-    for h in range(group):
-        for s in range(splits):
-            piece = (dq_acc[h * splits + s] * SCALE).astype(jnp.bfloat16)
-            dq_buf[s * block:(s + 1) * block, h * HEAD_WIDTH:(h + 1) * HEAD_WIDTH] = piece.T
-    send_out((1,))
 
     def drain(d, _):
         p = (me + d) % peers
@@ -355,8 +402,9 @@
             pltpu.VMEM((jobs, 1, block), f32),
             pltpu.VMEM((jobs, 1, block), f32),
             pltpu.VMEM((jobs, HEAD_WIDTH, block), f32),
+            pltpu.VMEM((jobs, HEAD_WIDTH, block), bf16),
             pltpu.VMEM((jobs, HEAD_WIDTH, block), f32),
-            pltpu.VMEM((2, chunk, HEAD_WIDTH), f32),
+            pltpu.VMEM((planes, 2, chunk, HEAD_WIDTH), f32),
             pltpu.VMEM((planes, 2, chunk, HEAD_WIDTH), bf16),
             pltpu.VMEM((planes, 2, chunk, HEAD_WIDTH), bf16),
             dma((8,)),
@@ -370,7 +418,7 @@
             dma((4, peers)),
         ],
         compiler_params=pltpu.CompilerParams(
-            collective_id=0, has_side_effects=True, vmem_limit_bytes=48 * 1024 * 1024
+            collective_id=0, has_side_effects=True, vmem_limit_bytes=60 * 1024 * 1024
         ),
     )(query, keys, values, output_gradient)
 

time: 82 us -> 72.2 us (0.88)
  Pallas kernels: 74.3 us -> 66.7 us
  local copies, waits for them, and re-layouts: 6.78 us -> 4.56 us
    pallas_call x1, Pallas kernels: 74.3 us -> 66.7 us  [shards(): pl.pallas_call(functools.partial(kernel, (tp, inner, planes, tok, group,...]
    unnamed x12 -> x10, local copies, waits for them, and re-layouts: 6.78 us -> 4.56 us
where the time goes in v2:
time: 72.2 us; the launch traced here: 71.9 us
  Pallas kernels  66.7 us (92%)
  local copies, waits for them, and re-layouts  4.56 us (6%)
    pallas_call x1, Pallas kernels, shards(): pl.pallas_call(functools.partial(kernel, (tp, inner, planes, tok, group,...  66.7 us
    unnamed x10, local copies, waits for them, and re-layouts  4.56 us

profile of v2, /device:TPU:0, one launch (start us, length us, event | category | flops | bytes accessed | tf_op | source)
XLA Modules:
  0.0 71.9 jit_solution(5281339062207938258)
XLA Ops:
  0.6 66.7 %shard_map.75 = (bf16[64,4096]{1,0:T(8,128)(2,1)}, bf16[64,4096]{1,0:T(8,128)(2,1)}, bf16[64,1024]{1,0:T(8,128)(2,1)}, bf16[64,1024]{1,0:T(8,128)(2,1)}) custom-call(bf16[64,4096]{1,0:T(8,128)(2,1)} %query.1, bf16[64,1024]{1,0:T(8,128)(2,1)} %keys.1, bf16[64,1024]{1,0:T(8,128)(2,1)} %values.1, bf16[64,4096]{1,0:T(8,128)(2,1)} %grads.1), custom_call_target="tpu_custom_call" | custom-call | tf_op jit(solution)/shard_map/pallas_call | solution.py:380
  67.3 0.0 copy-start
  67.4 1.9 %copy.12 = bf16[64,4096]{1,0:T(8,128)(2,1)} copy(bf16[64,4096]{1,0:T(8,128)(2,1)} %get-tuple-element.8) | data formatting | bytes 1048576
  69.3 0.0 copy-done
  69.3 0.0 copy-start.2
  69.3 0.8 %copy.13 = bf16[64,4096]{1,0:T(8,128)(2,1)} copy(bf16[64,4096]{1,0:T(8,128)(2,1)S(1)} %copy-done) | data formatting | bytes 1048576
  70.1 0.2 copy-done.2
  70.3 0.0 copy-start.1
  70.3 0.7 copy.14
  71.0 0.3 copy-done.1
  71.3 0.7 copy.15
Async XLA Ops:
  67.3 1.9 %copy-start = (bf16[64,4096]{1,0:T(8,128)(2,1)S(1)}, bf16[64,4096]{1,0:T(8,128)(2,1)}, u32[]{:S(2)}) copy-start(bf16[64,4096]{1,0:T(8,128)(2,1)} %get-tuple-element.9) | copy-start | bytes 1572868
  69.3 1.0 %copy-start.2 = (bf16[64,1024]{1,0:T(8,128)(2,1)S(1)}, bf16[64,1024]{1,0:T(8,128)(2,1)}, u32[]{:S(2)}) copy-start(bf16[64,1024]{1,0:T(8,128)(2,1)} %get-tuple-element.10) | copy-start | bytes 393220
  70.3 1.0 %copy-start.1 = (bf16[64,1024]{1,0:T(8,128)(2,1)S(1)}, bf16[64,1024]{1,0:T(8,128)(2,1)}, u32[]{:S(2)}) copy-start(bf16[64,1024]{1,0:T(8,128)(2,1)} %get-tuple-element.11) | copy-start | bytes 393220

commit v3 on v2

--- a/solution.py
+++ b/solution.py
@@ -25,7 +25,7 @@
     out_ref, dq_ref, dk_ref, dv_ref,
     q_all, g_all, kv_all, o_buf, dq_buf, fin,
     q_rows, q_cols, g_rows, g_cols, k_cols, v_cols,
-    row_max, row_sum, lse, delta, acc, o_cols, dq_acc, pair, part_out, part_in,
+    row_max, row_sum, lse, delta, acc, o_cols, dq_acc, p_all, ds_all, pair, part_out, part_in,
     own_sem, in_send, in_recv, kv_send, kv_recv, part_send, part_recv, out_send, out_recv,
 ):
     tp, inner, planes, tok, group, block = sizes
@@ -149,7 +149,7 @@
         for h in range(group):
             for s in range(splits):
                 piece = whole[s * block:(s + 1) * block, h * HEAD_WIDTH:(h + 1) * HEAD_WIDTH]
-                by_rows[h * splits + s] = piece
+                by_rows[(h * splits + s) * block:(h * splits + s + 1) * block] = piece
                 by_cols[h * splits + s] = piece.T
 
     await_in((2,))
@@ -174,7 +174,7 @@
             acc[i] = dot(v_cols[:, :seen], p.astype(jnp.bfloat16))
         return 0
 
-    lax.fori_loop(0, group, first, 0)
+    lax.fori_loop(0, group, first, 0, unroll=2)
 
     def take_grads():
         await_in((3,))
@@ -208,7 +208,7 @@
             acc[i] = acc[i] * shrink + dot(v_cols[...], p.astype(jnp.bfloat16))
             return 0
 
-        lax.fori_loop(0, jobs, one, 0)
+        lax.fori_loop(0, jobs, one, 0, unroll=4)
         return 0
 
     lax.fori_loop(0, plane, forward, 0)
@@ -264,18 +264,22 @@
         )
 
     def gradients(j, i, seen, split):
+        where = pl.ds(i * block if isinstance(i, int) else pl.multiple_of(i * block, block), block)
         s = dot(kv_all[j, 0, :seen], q_cols[i])
         if split is not None:
             s = masked(s, split)
         p = jnp.exp2(s * LOG2_SCALE - lse[i])
         dp = dot(kv_all[j, 1, :seen], g_cols[i])
         ds = (p * (dp - delta[i])).astype(jnp.bfloat16)
-        pair[j, 1, :seen] += dot(p.astype(jnp.bfloat16), g_rows[i])
-        pair[j, 0, :seen] += dot(ds, q_rows[i])
+        p_all[:seen, where] = p.astype(jnp.bfloat16)
+        ds_all[:seen, where] = ds
+        if seen < chunk:
+            unseen = jnp.zeros((chunk - seen, block), jnp.bfloat16)
+            p_all[seen:, where] = unseen
+            ds_all[seen:, where] = unseen
         dq_acc[i] += dot(k_cols[:, :seen], ds)
 
     def backward(j, diagonal):
-        pair[j] = jnp.zeros(pair.shape[1:], jnp.float32)
         k_cols[...] = kv_all[j, 0].T
 
         def one(i, _):
@@ -288,9 +292,11 @@
             return 0
 
         if diagonal:
-            lax.fori_loop(0, group, triangle, 0)
+            lax.fori_loop(0, group, triangle, 0, unroll=2)
         else:
-            lax.fori_loop(0, jobs, one, 0)
+            lax.fori_loop(0, jobs, one, 0, unroll=4)
+        pair[j, 1] = dot(p_all[...], g_rows[...])
+        pair[j, 0] = dot(ds_all[...], q_rows[...])
 
     def earlier(j, _):
         backward(j, False)
@@ -359,6 +365,15 @@
         return 0
 
     lax.fori_loop(0, plane, sent, 0)
+
+
+def hand_over(*refs):
+    sem = refs[8]
+    copies = [pltpu.make_async_copy(refs[i], refs[4 + i], sem.at[i]) for i in range(4)]
+    for copy in copies:
+        copy.start()
+    for copy in copies:
+        copy.wait()
 
 
 def shards(query, keys, values, output_gradient):
@@ -375,15 +390,15 @@
     jobs = group * (chunk // block)
     wide = group * HEAD_WIDTH
     bf16, f32 = jnp.bfloat16, jnp.float32
-    hbm = pl.BlockSpec(memory_space=pl.ANY)
+    anywhere = pl.BlockSpec(memory_space=pl.ANY)
     dma = pltpu.SemaphoreType.DMA
-    return pl.pallas_call(
+    results = pl.pallas_call(
         functools.partial(kernel, (tp, inner, planes, tok, group, block)),
         out_shape=tuple(
             jax.ShapeDtypeStruct(a.shape, a.dtype) for a in (query, query, keys, values)
         ),
-        in_specs=[hbm] * 4,
-        out_specs=(hbm,) * 4,
+        in_specs=[anywhere] * 4,
+        out_specs=(anywhere,) * 4,
         scratch_shapes=[
             pltpu.VMEM((chunk, wide), bf16),
             pltpu.VMEM((chunk, wide), bf16),
@@ -391,9 +406,9 @@
             pltpu.VMEM((chunk, wide), bf16),
             pltpu.VMEM((chunk, wide), bf16),
             pltpu.VMEM((2, chunk, HEAD_WIDTH), bf16),
-            pltpu.VMEM((jobs, block, HEAD_WIDTH), bf16),
+            pltpu.VMEM((jobs * block, HEAD_WIDTH), bf16),
             pltpu.VMEM((jobs, HEAD_WIDTH, block), bf16),
-            pltpu.VMEM((jobs, block, HEAD_WIDTH), bf16),
+            pltpu.VMEM((jobs * block, HEAD_WIDTH), bf16),
             pltpu.VMEM((jobs, HEAD_WIDTH, block), bf16),
             pltpu.VMEM((HEAD_WIDTH, chunk), bf16),
             pltpu.VMEM((HEAD_WIDTH, chunk), bf16),
@@ -404,6 +419,8 @@
             pltpu.VMEM((jobs, HEAD_WIDTH, block), f32),
             pltpu.VMEM((jobs, HEAD_WIDTH, block), bf16),
             pltpu.VMEM((jobs, HEAD_WIDTH, block), f32),
+            pltpu.VMEM((chunk, jobs * block), bf16),
+            pltpu.VMEM((chunk, jobs * block), bf16),
             pltpu.VMEM((planes, 2, chunk, HEAD_WIDTH), f32),
             pltpu.VMEM((planes, 2, chunk, HEAD_WIDTH), bf16),
             pltpu.VMEM((planes, 2, chunk, HEAD_WIDTH), bf16),
@@ -418,9 +435,17 @@
             dma((4, peers)),
         ],
         compiler_params=pltpu.CompilerParams(
-            collective_id=0, has_side_effects=True, vmem_limit_bytes=60 * 1024 * 1024
+            collective_id=0, has_side_effects=True, vmem_limit_bytes=64 * 1024 * 1024
         ),
     )(query, keys, values, output_gradient)
+    return pl.pallas_call(
+        hand_over,
+        out_shape=tuple(jax.ShapeDtypeStruct(a.shape, a.dtype) for a in results),
+        in_specs=[anywhere] * 4,
+        out_specs=(anywhere,) * 4,
+        scratch_shapes=[dma((4,))],
+        compiler_params=pltpu.CompilerParams(vmem_limit_bytes=64 * 1024 * 1024),
+    )(*results)
 
 
 def solution(mesh):

time: 72.2 us -> 108 us (1.50)
  Pallas kernels: 66.7 us -> 107 us
  local copies, waits for them, and re-layouts: 4.56 us -> 0 us
    pallas_call x0 -> x1, Pallas kernels: none -> 40.8 us  [shards(): pl.pallas_call(hand_over, out_shape=tuple((jax.ShapeDtypeStruct(a.shape,...]
    unnamed x10 -> x0, local copies, waits for them, and re-layouts: 4.56 us -> none
where the time goes in v3:
time: 108 us
  Pallas kernels  107 us (99%)
    pallas_call x1, Pallas kernels, shards(): pl.pallas_call(functools.partial(kernel, (tp, inner, planes, tok, group,...  66.2 us
    pallas_call x1, Pallas kernels, shards(): pl.pallas_call(hand_over, out_shape=tuple((jax.ShapeDtypeStruct(a.shape,...  40.8 us

profile of v3, /device:TPU:0, one launch (start us, length us, event | category | flops | bytes accessed | tf_op | source)
XLA Modules:
  0.0 107.7 jit_solution(13604206137556059206)
XLA Ops:
  0.6 66.2 %shard_map.75 = (bf16[64,4096]{1,0:T(8,128)(2,1)}, bf16[64,4096]{1,0:T(8,128)(2,1)}, bf16[64,1024]{1,0:T(8,128)(2,1)}, bf16[64,1024]{1,0:T(8,128)(2,1)}) custom-call(bf16[64,4096]{1,0:T(8,128)(2,1)} %query.1, bf16[64,1024]{1,0:T(8,128)(2,1)} %keys.1, bf16[64,1024]{1,0:T(8,128)(2,1)} %values.1, bf16[64,4096]{1,0:T(8,128)(2,1)} %grads.1), custom_call_target="tpu_custom_call" | custom-call | tf_op jit(solution)/shard_map/pallas_call | solution.py:395
  66.9 40.8 %shard_map.76 = (bf16[64,4096]{1,0:T(8,128)(2,1)}, bf16[64,4096]{1,0:T(8,128)(2,1)}, bf16[64,1024]{1,0:T(8,128)(2,1)}, bf16[64,1024]{1,0:T(8,128)(2,1)}) custom-call(bf16[64,4096]{1,0:T(8,128)(2,1)} %get-tuple-element.8.refs_0_, bf16[64,4096]{1,0:T(8,128)(2,1)} %get-tuple-element.9.refs_1_, bf16[64,1024]{1,0:T(8,128)(2,1)} %get-tuple-element.10.refs_2_, ...), custom_call_target="tpu_custom_call" | custom-call | tf_op jit(solution)/shard_map/pallas_call | solution.py:441

commit v4 on v3

--- a/solution.py
+++ b/solution.py
@@ -120,8 +120,6 @@
     for a in range(4):
         own_copy(a).start()
     send_in((0, 1))
-    send_in((2,))
-    send_in((3,))
 
     def kv_copy(j, target):
         return pltpu.make_async_remote_copy(
@@ -137,6 +135,17 @@
     def _():
         kv_copy(plane, plane + 1).start()
 
+    send_in((2,))
+
+    def left(d, _):
+        in_copy(2, me, (me + d) % peers).wait_send()
+        return 0
+
+    lax.fori_loop(1, peers, left, 0)
+    send_in((3,))
+
+    @pl.when(plane < planes - 1)
+    def _():
         def relay(n, _):
             j = plane - 1 - n
             kv_copy(j, plane).wait_recv()
@@ -342,8 +351,9 @@
 
     def drain(d, _):
         p = (me + d) % peers
+        for a in (0, 1, 3):
+            in_copy(a, me, p).wait_send()
         for a in range(4):
-            in_copy(a, me, p).wait_send()
             out_copy(a, me, p).wait_send()
             out_copy(a, p, me).wait_recv()
         return 0
@@ -368,12 +378,16 @@
 
 
 def hand_over(*refs):
-    sem = refs[8]
-    copies = [pltpu.make_async_copy(refs[i], refs[4 + i], sem.at[i]) for i in range(4)]
-    for copy in copies:
-        copy.start()
-    for copy in copies:
-        copy.wait()
+    sources, results, held, sem = refs[:4], refs[4:8], refs[8:12], refs[12]
+    loads = [pltpu.make_async_copy(sources[i], held[i], sem.at[0, i]) for i in range(4)]
+    stores = [pltpu.make_async_copy(held[i], results[i], sem.at[1, i]) for i in range(4)]
+    for load in loads:
+        load.start()
+    for load, store in zip(loads, stores):
+        load.wait()
+        store.start()
+    for store in stores:
+        store.wait()
 
 
 def shards(query, keys, values, output_gradient):
@@ -443,7 +457,7 @@
         out_shape=tuple(jax.ShapeDtypeStruct(a.shape, a.dtype) for a in results),
         in_specs=[anywhere] * 4,
         out_specs=(anywhere,) * 4,
-        scratch_shapes=[dma((4,))],
+        scratch_shapes=[pltpu.VMEM(a.shape, a.dtype) for a in results] + [dma((2, 4))],
         compiler_params=pltpu.CompilerParams(vmem_limit_bytes=64 * 1024 * 1024),
     )(*results)
 

time: 108 us -> 68.9 us (0.64)
  Pallas kernels: 107 us -> 68 us
    pallas_call x1, Pallas kernels: 40.8 us -> 2.16 us  [shards(): pl.pallas_call(hand_over, out_shape=tuple((jax.ShapeDtypeStruct(a.shape,...]
where the time goes in v4:
time: 68.9 us; the launch traced here: 68.6 us
  Pallas kernels  68 us (99%)
    pallas_call x1, Pallas kernels, shards(): pl.pallas_call(functools.partial(kernel, (tp, inner, planes, tok, group,...  65.8 us
    pallas_call x1, Pallas kernels, shards(): pl.pallas_call(hand_over, out_shape=tuple((jax.ShapeDtypeStruct(a.shape,...  2.16 us

profile of v4, /device:TPU:0, one launch (start us, length us, event | category | flops | bytes accessed | tf_op | source)
XLA Modules:
  0.0 68.6 jit_solution(10319381214053397632)
XLA Ops:
  0.6 65.8 %shard_map.75 = (bf16[64,4096]{1,0:T(8,128)(2,1)}, bf16[64,4096]{1,0:T(8,128)(2,1)}, bf16[64,1024]{1,0:T(8,128)(2,1)}, bf16[64,1024]{1,0:T(8,128)(2,1)}) custom-call(bf16[64,4096]{1,0:T(8,128)(2,1)} %query.1, bf16[64,1024]{1,0:T(8,128)(2,1)} %keys.1, bf16[64,1024]{1,0:T(8,128)(2,1)} %values.1, bf16[64,4096]{1,0:T(8,128)(2,1)} %grads.1), custom_call_target="tpu_custom_call" | custom-call | tf_op jit(solution)/shard_map/pallas_call | solution.py:409
  66.5 2.2 %shard_map.76 = (bf16[64,4096]{1,0:T(8,128)(2,1)}, bf16[64,4096]{1,0:T(8,128)(2,1)}, bf16[64,1024]{1,0:T(8,128)(2,1)}, bf16[64,1024]{1,0:T(8,128)(2,1)}) custom-call(bf16[64,4096]{1,0:T(8,128)(2,1)} %get-tuple-element.8.refs_0_, bf16[64,4096]{1,0:T(8,128)(2,1)} %get-tuple-element.9.refs_1_, bf16[64,1024]{1,0:T(8,128)(2,1)} %get-tuple-element.10.refs_2_, ...), custom_call_target="tpu_custom_call" | custom-call | tf_op jit(solution)/shard_map/pallas_call | solution.py:455

commit v5 on v4

--- a/solution.py
+++ b/solution.py
@@ -26,7 +26,7 @@
     q_all, g_all, kv_all, o_buf, dq_buf, fin,
     q_rows, q_cols, g_rows, g_cols, k_cols, v_cols,
     row_max, row_sum, lse, delta, acc, o_cols, dq_acc, p_all, ds_all, pair, part_out, part_in,
-    own_sem, in_send, in_recv, kv_send, kv_recv, part_send, part_recv, out_send, out_recv,
+    own_sem, in_send, in_recv, kv_send, kv_recv, part_send, part_recv, out_send, out_recv, turn_sem,
 ):
     tp, inner, planes, tok, group, block = sizes
     peers = tp * inner
@@ -131,28 +131,55 @@
     await_in((0, 1))
     top_plane = plane == planes - 1
 
-    @pl.when(plane < planes - 1)
-    def _():
-        kv_copy(plane, plane + 1).start()
-
-    send_in((2,))
-
-    def left(d, _):
-        in_copy(2, me, (me + d) % peers).wait_send()
-        return 0
-
-    lax.fori_loop(1, peers, left, 0)
-    send_in((3,))
-
-    @pl.when(plane < planes - 1)
-    def _():
-        def relay(n, _):
+    staged = inner % 2 == 0
+    leads = lane % 2 == 0 if staged else lane == lane
+    below = plane < planes - 1
+
+    def relay():
+        def one(n, _):
             j = plane - 1 - n
             kv_copy(j, plane).wait_recv()
             kv_copy(j, plane + 1).start()
             return 0
 
-        lax.fori_loop(0, plane, relay, 0)
+        lax.fori_loop(0, plane, one, 0)
+
+    @pl.when(below & leads)
+    def _():
+        kv_copy(plane, plane + 1).start()
+
+    send_in((2,))
+
+    @pl.when(top_plane)
+    def _():
+        def left(d, _):
+            in_copy(2, me, (me + d) % peers).wait_send()
+            return 0
+
+        lax.fori_loop(1, peers, left, 0)
+
+    send_in((3,))
+
+    @pl.when(below & leads)
+    def _():
+        relay()
+
+        def gone(j, _):
+            kv_copy(j, plane + 1).wait_send()
+            return 0
+
+        lax.fori_loop(0, plane + 1, gone, 0)
+        if staged:
+            pl.semaphore_signal(
+                turn_sem, inc=1, device_id=(ctx_index + 1, tp_index), device_id_type=MESH
+            )
+
+    if staged:
+        @pl.when(below & (lane % 2 == 1))
+        def _():
+            pl.semaphore_wait(turn_sem, 1)
+            kv_copy(plane, plane + 1).start()
+            relay()
 
     def spread(whole, by_rows, by_cols):
         for h in range(group):
@@ -353,6 +380,11 @@
         p = (me + d) % peers
         for a in (0, 1, 3):
             in_copy(a, me, p).wait_send()
+
+        @pl.when(below)
+        def _():
+            in_copy(2, me, p).wait_send()
+
         for a in range(4):
             out_copy(a, me, p).wait_send()
             out_copy(a, p, me).wait_recv()
@@ -362,13 +394,14 @@
     for a in range(4):
         own_out(a).wait()
 
-    @pl.when(plane < planes - 1)
-    def _():
-        def one(j, _):
-            kv_copy(j, plane + 1).wait_send()
-            return 0
-
-        lax.fori_loop(0, plane + 1, one, 0)
+    if staged:
+        @pl.when(below & (lane % 2 == 1))
+        def _():
+            def one(j, _):
+                kv_copy(j, plane + 1).wait_send()
+                return 0
+
+            lax.fori_loop(0, plane + 1, one, 0)
 
     def sent(j, _):
         part_copy(j, plane - 1).wait_send()
@@ -447,6 +480,7 @@
             dma((planes,)),
             dma((4, peers)),
             dma((4, peers)),
+            pltpu.SemaphoreType.REGULAR,
         ],
         compiler_params=pltpu.CompilerParams(
             collective_id=0, has_side_effects=True, vmem_limit_bytes=64 * 1024 * 1024

time: 68.9 us -> 68.5 us (level)
  no operation moved by 1% of the time
where the time goes in v5:
time: 68.5 us; the launch traced here: 68.3 us
  Pallas kernels  67.7 us (99%)
    pallas_call x1, Pallas kernels, shards(): pl.pallas_call(functools.partial(kernel, (tp, inner, planes, tok, group,...  65.5 us
    pallas_call x1, Pallas kernels, shards(): pl.pallas_call(hand_over, out_shape=tuple((jax.ShapeDtypeStruct(a.shape,...  2.16 us

profile of v5, /device:TPU:0, one launch (start us, length us, event | category | flops | bytes accessed | tf_op | source)
XLA Modules:
  0.0 68.3 jit_solution(1165839599612985458)
XLA Ops:
  0.6 65.5 %shard_map.75 = (bf16[64,4096]{1,0:T(8,128)(2,1)}, bf16[64,4096]{1,0:T(8,128)(2,1)}, bf16[64,1024]{1,0:T(8,128)(2,1)}, bf16[64,1024]{1,0:T(8,128)(2,1)}) custom-call(bf16[64,4096]{1,0:T(8,128)(2,1)} %query.1, bf16[64,1024]{1,0:T(8,128)(2,1)} %keys.1, bf16[64,1024]{1,0:T(8,128)(2,1)} %values.1, bf16[64,4096]{1,0:T(8,128)(2,1)} %grads.1), custom_call_target="tpu_custom_call" | custom-call | tf_op jit(solution)/shard_map/pallas_call | solution.py:442
  66.1 2.2 %shard_map.76 = (bf16[64,4096]{1,0:T(8,128)(2,1)}, bf16[64,4096]{1,0:T(8,128)(2,1)}, bf16[64,1024]{1,0:T(8,128)(2,1)}, bf16[64,1024]{1,0:T(8,128)(2,1)}) custom-call(bf16[64,4096]{1,0:T(8,128)(2,1)} %get-tuple-element.8.refs_0_, bf16[64,4096]{1,0:T(8,128)(2,1)} %get-tuple-element.9.refs_1_, bf16[64,1024]{1,0:T(8,128)(2,1)} %get-tuple-element.10.refs_2_, ...), custom_call_target="tpu_custom_call" | custom-call | tf_op jit(solution)/shard_map/pallas_call | solution.py:489

commit v6 on v5

--- a/solution.py
+++ b/solution.py
@@ -21,12 +21,14 @@
 
 def kernel(
     sizes,
+    query_hbm, keys_hbm, values_hbm, grads_hbm,
+    out_hbm, dq_hbm, dk_hbm, dv_hbm,
     query, keys, values, grads,
     out_ref, dq_ref, dk_ref, dv_ref,
     q_all, g_all, kv_all, o_buf, dq_buf, fin,
     q_rows, q_cols, g_rows, g_cols, k_cols, v_cols,
     row_max, row_sum, lse, delta, acc, o_cols, dq_acc, p_all, ds_all, pair, part_out, part_in,
-    own_sem, in_send, in_recv, kv_send, kv_recv, part_send, part_recv, out_send, out_recv, turn_sem,
+    own_sem, in_send, in_recv, kv_send, kv_recv, part_send, part_recv, out_send, out_recv, load_sem, turn_sem,
 ):
     tp, inner, planes, tok, group, block = sizes
     peers = tp * inner
@@ -46,6 +48,15 @@
     def plane_id(z):
         return (z * inner + lane, tp_index)
 
+    loads = [
+        pltpu.make_async_copy(src, dst, load_sem.at[n])
+        for n, (src, dst) in enumerate(
+            ((keys_hbm, keys), (values_hbm, values), (query_hbm, query), (grads_hbm, grads))
+        )
+    ]
+    for load in loads:
+        load.start()
+
     barrier = pltpu.get_barrier_semaphore()
 
     def greet(d, _):
@@ -117,6 +128,8 @@
 
         lax.fori_loop(1, peers, one, 0)
 
+    for load in loads:
+        load.wait()
     for a in range(4):
         own_copy(a).start()
     send_in((0, 1))
@@ -393,6 +406,14 @@
     lax.fori_loop(1, peers, drain, 0)
     for a in range(4):
         own_out(a).wait()
+    stores = [
+        pltpu.make_async_copy(src, dst, load_sem.at[4 + n])
+        for n, (src, dst) in enumerate(
+            ((out_ref, out_hbm), (dq_ref, dq_hbm), (dk_ref, dk_hbm), (dv_ref, dv_hbm))
+        )
+    ]
+    for store in stores:
+        store.start()
 
     if staged:
         @pl.when(below & (lane % 2 == 1))
@@ -408,6 +429,8 @@
         return 0
 
     lax.fori_loop(0, plane, sent, 0)
+    for store in stores:
+        store.wait()
 
 
 def hand_over(*refs):
@@ -447,6 +470,9 @@
         in_specs=[anywhere] * 4,
         out_specs=(anywhere,) * 4,
         scratch_shapes=[
+            pltpu.VMEM(a.shape, a.dtype)
+            for a in (query, keys, values, output_gradient, query, query, keys, values)
+        ] + [
             pltpu.VMEM((chunk, wide), bf16),
             pltpu.VMEM((chunk, wide), bf16),
             pltpu.VMEM((planes, 2, chunk, HEAD_WIDTH), bf16),
@@ -480,6 +506,7 @@
             dma((planes,)),
             dma((4, peers)),
             dma((4, peers)),
+            dma((8,)),
             pltpu.SemaphoreType.REGULAR,
         ],
         compiler_params=pltpu.CompilerParams(

time: 68.5 us -> 69.4 us (1.013)
  Pallas kernels: 67.7 us -> 68.6 us
    pallas_call x1, Pallas kernels: 65.5 us -> 66.5 us  [shards(): pl.pallas_call(functools.partial(kernel, (tp, inner, planes, tok, group,...]
where the time goes in v6:
time: 69.4 us; the launch traced here: 69.3 us
  Pallas kernels  68.6 us (99%)
    pallas_call x1, Pallas kernels, shards(): pl.pallas_call(functools.partial(kernel, (tp, inner, planes, tok, group,...  66.5 us
    pallas_call x1, Pallas kernels, shards(): pl.pallas_call(hand_over, out_shape=tuple((jax.ShapeDtypeStruct(a.shape,...  2.16 us

profile of v6, /device:TPU:0, one launch (start us, length us, event | category | flops | bytes accessed | tf_op | source)
XLA Modules:
  0.0 69.3 jit_solution(17846149049443843441)
XLA Ops:
  0.6 66.5 %shard_map.75 = (bf16[64,4096]{1,0:T(8,128)(2,1)}, bf16[64,4096]{1,0:T(8,128)(2,1)}, bf16[64,1024]{1,0:T(8,128)(2,1)}, bf16[64,1024]{1,0:T(8,128)(2,1)}) custom-call(bf16[64,4096]{1,0:T(8,128)(2,1)} %query_hbm.1, bf16[64,1024]{1,0:T(8,128)(2,1)} %keys_hbm.1, bf16[64,1024]{1,0:T(8,128)(2,1)} %values_hbm.1, bf16[64,4096]{1,0:T(8,128)(2,1)} %grads_hbm.1), custom_call_target="tpu_custom_call" | custom-call | tf_op jit(solution)/shard_map/pallas_call | solution.py:465
  67.1 2.2 %shard_map.76 = (bf16[64,4096]{1,0:T(8,128)(2,1)}, bf16[64,4096]{1,0:T(8,128)(2,1)}, bf16[64,1024]{1,0:T(8,128)(2,1)}, bf16[64,1024]{1,0:T(8,128)(2,1)}) custom-call(bf16[64,4096]{1,0:T(8,128)(2,1)} %get-tuple-element.8.refs_0_, bf16[64,4096]{1,0:T(8,128)(2,1)} %get-tuple-element.9.refs_1_, bf16[64,1024]{1,0:T(8,128)(2,1)} %get-tuple-element.10.refs_2_, ...), custom_call_target="tpu_custom_call" | custom-call | tf_op jit(solution)/shard_map/pallas_call | solution.py:516

commit v7 on v5

--- a/solution.py
+++ b/solution.py
@@ -25,7 +25,7 @@
     out_ref, dq_ref, dk_ref, dv_ref,
     q_all, g_all, kv_all, o_buf, dq_buf, fin,
     q_rows, q_cols, g_rows, g_cols, k_cols, v_cols,
-    row_max, row_sum, lse, delta, acc, o_cols, dq_acc, p_all, ds_all, pair, part_out, part_in,
+    row_max, row_sum, lse, delta, acc, o_cols, dq_acc, p_all, ds_all, s_all, dp_all, pair, part_out, part_in,
     own_sem, in_send, in_recv, kv_send, kv_recv, part_send, part_recv, out_send, out_recv, turn_sem,
 ):
     tp, inner, planes, tok, group, block = sizes
@@ -202,9 +202,9 @@
     def first(h, _):
         for split in range(splits):
             i, seen = h * splits + split, (split + 1) * block
-            s = masked(dot(kv_all[plane, 0, :seen], q_cols[i]), split)
+            s = masked(dot(kv_all[plane, 0, :seen], q_cols[i]) * LOG2_SCALE, split)
             top = jnp.max(s, axis=0, keepdims=True)
-            p = jnp.exp2((s - top) * LOG2_SCALE)
+            p = jnp.exp2(s - top)
             row_max[i] = top
             row_sum[i] = jnp.sum(p, axis=0, keepdims=True)
             acc[i] = dot(v_cols[:, :seen], p.astype(jnp.bfloat16))
@@ -212,20 +212,11 @@
 
     lax.fori_loop(0, group, first, 0, unroll=2)
 
-    def take_grads():
-        await_in((3,))
-        spread(g_all, g_rows, g_cols)
-
-    @pl.when(plane == 0)
-    def _():
-        take_grads()
+    await_in((3,))
+    spread(g_all, g_rows, g_cols)
 
     def forward(n, _):
         j = plane - 1 - n
-
-        @pl.when(j == 0)
-        def _():
-            take_grads()
 
         @pl.when(top_plane)
         def _():
@@ -234,11 +225,13 @@
         v_cols[...] = kv_all[j, 1].T
 
         def one(i, _):
-            s = dot(kv_all[j, 0], q_cols[i])
+            s = dot(kv_all[j, 0], q_cols[i]) * LOG2_SCALE
+            s_all[j, i] = s
+            dp_all[j, i] = dot(kv_all[j, 1], g_cols[i])
             old = row_max[i]
             top = jnp.maximum(old, jnp.max(s, axis=0, keepdims=True))
-            p = jnp.exp2((s - top) * LOG2_SCALE)
-            shrink = jnp.exp2((old - top) * LOG2_SCALE)
+            p = jnp.exp2(s - top)
+            shrink = jnp.exp2(old - top)
             row_max[i] = top
             row_sum[i] = row_sum[i] * shrink + jnp.sum(p, axis=0, keepdims=True)
             acc[i] = acc[i] * shrink + dot(v_cols[...], p.astype(jnp.bfloat16))
@@ -253,7 +246,7 @@
         total = row_sum[i]
         rounded = (acc[i] / total).astype(jnp.bfloat16)
         o_cols[i] = rounded
-        lse[i] = row_max[i] * LOG2_SCALE + jnp.log2(total)
+        lse[i] = row_max[i] + jnp.log2(total)
         delta[i] = jnp.sum(
             g_cols[i].astype(jnp.float32) * rounded.astype(jnp.float32), axis=0, keepdims=True
         )
@@ -301,11 +294,12 @@
 
     def gradients(j, i, seen, split):
         where = pl.ds(i * block if isinstance(i, int) else pl.multiple_of(i * block, block), block)
-        s = dot(kv_all[j, 0, :seen], q_cols[i])
         if split is not None:
-            s = masked(s, split)
-        p = jnp.exp2(s * LOG2_SCALE - lse[i])
-        dp = dot(kv_all[j, 1, :seen], g_cols[i])
+            s = masked(dot(kv_all[j, 0, :seen], q_cols[i]) * LOG2_SCALE, split)
+            dp = dot(kv_all[j, 1, :seen], g_cols[i])
+        else:
+            s, dp = s_all[j, i], dp_all[j, i]
+        p = jnp.exp2(s - lse[i])
         ds = (p * (dp - delta[i])).astype(jnp.bfloat16)
         p_all[:seen, where] = p.astype(jnp.bfloat16)
         ds_all[:seen, where] = ds
@@ -468,6 +462,8 @@
             pltpu.VMEM((jobs, HEAD_WIDTH, block), f32),
             pltpu.VMEM((chunk, jobs * block), bf16),
             pltpu.VMEM((chunk, jobs * block), bf16),
+            pltpu.VMEM((max(planes - 1, 1), jobs, chunk, block), f32),
+            pltpu.VMEM((max(planes - 1, 1), jobs, chunk, block), f32),
             pltpu.VMEM((planes, 2, chunk, HEAD_WIDTH), f32),
             pltpu.VMEM((planes, 2, chunk, HEAD_WIDTH), bf16),
             pltpu.VMEM((planes, 2, chunk, HEAD_WIDTH), bf16),

time: 68.5 us -> 65.1 us (0.950)
  Pallas kernels: 67.7 us -> 64.1 us
    pallas_call x1, Pallas kernels: 65.5 us -> 62 us  [shards(): pl.pallas_call(functools.partial(kernel, (tp, inner, planes, tok, group,...]
where the time goes in v7:
time: 65.1 us; the launch traced here: 64.8 us
  Pallas kernels  64.1 us (98%)
    pallas_call x1, Pallas kernels, shards(): pl.pallas_call(functools.partial(kernel, (tp, inner, planes, tok, group,...  62 us
    pallas_call x1, Pallas kernels, shards(): pl.pallas_call(hand_over, out_shape=tuple((jax.ShapeDtypeStruct(a.shape,...  2.16 us

profile of v7, /device:TPU:0, one launch (start us, length us, event | category | flops | bytes accessed | tf_op | source)
XLA Modules:
  0.0 64.8 jit_solution(14708936557427294780)
XLA Ops:
  0.6 62.0 %shard_map.75 = (bf16[64,4096]{1,0:T(8,128)(2,1)}, bf16[64,4096]{1,0:T(8,128)(2,1)}, bf16[64,1024]{1,0:T(8,128)(2,1)}, bf16[64,1024]{1,0:T(8,128)(2,1)}) custom-call(bf16[64,4096]{1,0:T(8,128)(2,1)} %query.1, bf16[64,1024]{1,0:T(8,128)(2,1)} %keys.1, bf16[64,1024]{1,0:T(8,128)(2,1)} %values.1, bf16[64,4096]{1,0:T(8,128)(2,1)} %grads.1), custom_call_target="tpu_custom_call" | custom-call | tf_op jit(solution)/shard_map/pallas_call | solution.py:436
  62.6 2.2 %shard_map.76 = (bf16[64,4096]{1,0:T(8,128)(2,1)}, bf16[64,4096]{1,0:T(8,128)(2,1)}, bf16[64,1024]{1,0:T(8,128)(2,1)}, bf16[64,1024]{1,0:T(8,128)(2,1)}) custom-call(bf16[64,4096]{1,0:T(8,128)(2,1)} %get-tuple-element.8.refs_0_, bf16[64,4096]{1,0:T(8,128)(2,1)} %get-tuple-element.9.refs_1_, bf16[64,1024]{1,0:T(8,128)(2,1)} %get-tuple-element.10.refs_2_, ...), custom_call_target="tpu_custom_call" | custom-call | tf_op jit(solution)/shard_map/pallas_call | solution.py:485

commit v8 on v7

--- a/solution.py
+++ b/solution.py
@@ -121,10 +121,10 @@
         own_copy(a).start()
     send_in((0, 1))
 
-    def kv_copy(j, target):
+    def kv_copy(j, half, target):
         return pltpu.make_async_remote_copy(
-            src_ref=kv_all.at[j], dst_ref=kv_all.at[j],
-            send_sem=kv_send.at[j], recv_sem=kv_recv.at[j],
+            src_ref=kv_all.at[j, half], dst_ref=kv_all.at[j, half],
+            send_sem=kv_send.at[j, half], recv_sem=kv_recv.at[j, half],
             device_id=plane_id(target), device_id_type=MESH,
         )
 
@@ -138,15 +138,17 @@
     def relay():
         def one(n, _):
             j = plane - 1 - n
-            kv_copy(j, plane).wait_recv()
-            kv_copy(j, plane + 1).start()
+            for half in range(2):
+                kv_copy(j, half, plane).wait_recv()
+                kv_copy(j, half, plane + 1).start()
             return 0
 
         lax.fori_loop(0, plane, one, 0)
 
     @pl.when(below & leads)
     def _():
-        kv_copy(plane, plane + 1).start()
+        for half in range(2):
+            kv_copy(plane, half, plane + 1).start()
 
     send_in((2,))
 
@@ -165,7 +167,8 @@
         relay()
 
         def gone(j, _):
-            kv_copy(j, plane + 1).wait_send()
+            for half in range(2):
+                kv_copy(j, half, plane + 1).wait_send()
             return 0
 
         lax.fori_loop(0, plane + 1, gone, 0)
@@ -178,7 +181,8 @@
         @pl.when(below & (lane % 2 == 1))
         def _():
             pl.semaphore_wait(turn_sem, 1)
-            kv_copy(plane, plane + 1).start()
+            for half in range(2):
+                kv_copy(plane, half, plane + 1).start()
             relay()
 
     def spread(whole, by_rows, by_cols):
@@ -203,6 +207,7 @@
         for split in range(splits):
             i, seen = h * splits + split, (split + 1) * block
             s = masked(dot(kv_all[plane, 0, :seen], q_cols[i]) * LOG2_SCALE, split)
+            s_all[plane, i, :seen] = s
             top = jnp.max(s, axis=0, keepdims=True)
             p = jnp.exp2(s - top)
             row_max[i] = top
@@ -215,12 +220,21 @@
     await_in((3,))
     spread(g_all, g_rows, g_cols)
 
+    def first_dp(h, _):
+        for split in range(splits):
+            i, seen = h * splits + split, (split + 1) * block
+            dp_all[plane, i, :seen] = dot(kv_all[plane, 1, :seen], g_cols[i])
+        return 0
+
+    lax.fori_loop(0, group, first_dp, 0, unroll=2)
+
     def forward(n, _):
         j = plane - 1 - n
 
         @pl.when(top_plane)
         def _():
-            kv_copy(j, plane).wait_recv()
+            for half in range(2):
+                kv_copy(j, half, plane).wait_recv()
 
         v_cols[...] = kv_all[j, 1].T
 
@@ -285,22 +299,17 @@
 
     dq_acc[...] = jnp.zeros_like(dq_acc)
 
-    def part_copy(j, target):
+    def part_copy(j, half, target):
         return pltpu.make_async_remote_copy(
-            src_ref=part_out.at[j], dst_ref=part_in.at[j],
-            send_sem=part_send.at[j], recv_sem=part_recv.at[j],
+            src_ref=part_out.at[j, half], dst_ref=part_in.at[j, half],
+            send_sem=part_send.at[j, half], recv_sem=part_recv.at[j, half],
             device_id=plane_id(target), device_id_type=MESH,
         )
 
-    def gradients(j, i, seen, split):
+    def gradients(j, i, seen):
         where = pl.ds(i * block if isinstance(i, int) else pl.multiple_of(i * block, block), block)
-        if split is not None:
-            s = masked(dot(kv_all[j, 0, :seen], q_cols[i]) * LOG2_SCALE, split)
-            dp = dot(kv_all[j, 1, :seen], g_cols[i])
-        else:
-            s, dp = s_all[j, i], dp_all[j, i]
-        p = jnp.exp2(s - lse[i])
-        ds = (p * (dp - delta[i])).astype(jnp.bfloat16)
+        p = jnp.exp2(s_all[j, i, :seen] - lse[i])
+        ds = (p * (dp_all[j, i, :seen] - delta[i])).astype(jnp.bfloat16)
         p_all[:seen, where] = p.astype(jnp.bfloat16)
         ds_all[:seen, where] = ds
         if seen < chunk:
@@ -313,29 +322,28 @@
         k_cols[...] = kv_all[j, 0].T
 
         def one(i, _):
-            gradients(j, i, chunk, None)
+            gradients(j, i, chunk)
             return 0
 
         def triangle(h, _):
             for split in range(splits):
-                gradients(j, h * splits + split, (split + 1) * block, split)
+                gradients(j, h * splits + split, (split + 1) * block)
             return 0
 
         if diagonal:
             lax.fori_loop(0, group, triangle, 0, unroll=2)
         else:
             lax.fori_loop(0, jobs, one, 0, unroll=4)
-        pair[j, 1] = dot(p_all[...], g_rows[...])
-        pair[j, 0] = dot(ds_all[...], q_rows[...])
+        for half, weights, lines in ((1, p_all, g_rows), (0, ds_all, q_rows)):
+            pair[j, half] = dot(weights[...], lines[...])
+            if not diagonal:
+                @pl.when(top_plane)
+                def _():
+                    part_out[j, half] = pair[j, half].astype(jnp.bfloat16)
+                    part_copy(j, half, plane - 1).start()
 
     def earlier(j, _):
         backward(j, False)
-
-        @pl.when(top_plane)
-        def _():
-            part_out[j] = pair[j].astype(jnp.bfloat16)
-            part_copy(j, plane - 1).start()
-
         return 0
 
     lax.fori_loop(0, plane, earlier, 0)
@@ -354,21 +362,26 @@
     gather_cols(dq_acc, dq_buf, SCALE)
     send_out((1,))
 
-    @pl.when(plane < planes - 1)
+    @pl.when(below)
     def _():
         def chain(j, _):
-            part_copy(j, plane).wait_recv()
-            part_out[j] = (pair[j] + part_in[j].astype(jnp.float32)).astype(jnp.bfloat16)
-            part_copy(j, plane - 1).start()
+            for half in (1, 0):
+                part_copy(j, half, plane).wait_recv()
+                whole = pair[j, half] + part_in[j, half].astype(jnp.float32)
+                part_out[j, half] = whole.astype(jnp.bfloat16)
+                part_copy(j, half, plane - 1).start()
             return 0
 
         lax.fori_loop(0, plane, chain, 0)
-        part_copy(plane, plane).wait_recv()
-        pair[plane] += part_in[plane].astype(jnp.float32)
-
-    fin[0] = (pair[plane, 0] * SCALE).astype(jnp.bfloat16)
-    fin[1] = pair[plane, 1].astype(jnp.bfloat16)
-    send_out((2, 3))
+
+    for half, factor in ((1, 1.0), (0, SCALE)):
+        @pl.when(below)
+        def _():
+            part_copy(plane, half, plane).wait_recv()
+            pair[plane, half] += part_in[plane, half].astype(jnp.float32)
+
+        fin[half] = (pair[plane, half] * factor).astype(jnp.bfloat16)
+        send_out((2 + half,))
 
     def drain(d, _):
         p = (me + d) % peers
@@ -392,13 +405,15 @@
         @pl.when(below & (lane % 2 == 1))
         def _():
             def one(j, _):
-                kv_copy(j, plane + 1).wait_send()
+                for half in range(2):
+                    kv_copy(j, half, plane + 1).wait_send()
                 return 0
 
             lax.fori_loop(0, plane + 1, one, 0)
 
     def sent(j, _):
-        part_copy(j, plane - 1).wait_send()
+        for half in range(2):
+            part_copy(j, half, plane - 1).wait_send()
         return 0
 
     lax.fori_loop(0, plane, sent, 0)
@@ -462,18 +477,18 @@
             pltpu.VMEM((jobs, HEAD_WIDTH, block), f32),
             pltpu.VMEM((chunk, jobs * block), bf16),
             pltpu.VMEM((chunk, jobs * block), bf16),
-            pltpu.VMEM((max(planes - 1, 1), jobs, chunk, block), f32),
-            pltpu.VMEM((max(planes - 1, 1), jobs, chunk, block), f32),
+            pltpu.VMEM((planes, jobs, chunk, block), f32),
+            pltpu.VMEM((planes, jobs, chunk, block), f32),
             pltpu.VMEM((planes, 2, chunk, HEAD_WIDTH), f32),
             pltpu.VMEM((planes, 2, chunk, HEAD_WIDTH), bf16),
             pltpu.VMEM((planes, 2, chunk, HEAD_WIDTH), bf16),
             dma((8,)),
             dma((4, peers)),
             dma((4, peers)),
-            dma((planes,)),
-            dma((planes,)),
-            dma((planes,)),
-            dma((planes,)),
+            dma((planes, 2)),
+            dma((planes, 2)),
+            dma((planes, 2)),
+            dma((planes, 2)),
             dma((4, peers)),
             dma((4, peers)),
             pltpu.SemaphoreType.REGULAR,

time: 65.1 us -> 64.2 us (0.986)
  the two profiles are of different devices: /device:TPU:0 before, /device:TPU:29 now
where the time goes in v8:
time: 64.2 us; the launch traced here: 64 us
  Pallas kernels  63.4 us (99%)
    pallas_call x1, Pallas kernels, shards(): pl.pallas_call(functools.partial(kernel, (tp, inner, planes, tok, group,...  61.2 us
    pallas_call x1, Pallas kernels, shards(): pl.pallas_call(hand_over, out_shape=tuple((jax.ShapeDtypeStruct(a.shape,...  2.16 us

profile of v8, /device:TPU:29, one launch (start us, length us, event | category | flops | bytes accessed | tf_op | source)
XLA Modules:
  0.0 64.0 jit_solution(3015409803977919609)
XLA Ops:
  0.6 61.2 %shard_map.75 = (bf16[64,4096]{1,0:T(8,128)(2,1)}, bf16[64,4096]{1,0:T(8,128)(2,1)}, bf16[64,1024]{1,0:T(8,128)(2,1)}, bf16[64,1024]{1,0:T(8,128)(2,1)}) custom-call(bf16[64,4096]{1,0:T(8,128)(2,1)} %query.1, bf16[64,1024]{1,0:T(8,128)(2,1)} %keys.1, bf16[64,1024]{1,0:T(8,128)(2,1)} %values.1, bf16[64,4096]{1,0:T(8,128)(2,1)} %grads.1), custom_call_target="tpu_custom_call" | custom-call | tf_op jit(solution)/shard_map/pallas_call | solution.py:451
  61.9 2.2 %shard_map.76 = (bf16[64,4096]{1,0:T(8,128)(2,1)}, bf16[64,4096]{1,0:T(8,128)(2,1)}, bf16[64,1024]{1,0:T(8,128)(2,1)}, bf16[64,1024]{1,0:T(8,128)(2,1)}) custom-call(bf16[64,4096]{1,0:T(8,128)(2,1)} %get-tuple-element.8.refs_0_, bf16[64,4096]{1,0:T(8,128)(2,1)} %get-tuple-element.9.refs_1_, bf16[64,1024]{1,0:T(8,128)(2,1)} %get-tuple-element.10.refs_2_, ...), custom_call_target="tpu_custom_call" | custom-call | tf_op jit(solution)/shard_map/pallas_call | solution.py:500

commit v9 on v8

--- a/solution.py
+++ b/solution.py
@@ -207,7 +207,6 @@
         for split in range(splits):
             i, seen = h * splits + split, (split + 1) * block
             s = masked(dot(kv_all[plane, 0, :seen], q_cols[i]) * LOG2_SCALE, split)
-            s_all[plane, i, :seen] = s
             top = jnp.max(s, axis=0, keepdims=True)
             p = jnp.exp2(s - top)
             row_max[i] = top
@@ -219,14 +218,6 @@
 
     await_in((3,))
     spread(g_all, g_rows, g_cols)
-
-    def first_dp(h, _):
-        for split in range(splits):
-            i, seen = h * splits + split, (split + 1) * block
-            dp_all[plane, i, :seen] = dot(kv_all[plane, 1, :seen], g_cols[i])
-        return 0
-
-    lax.fori_loop(0, group, first_dp, 0, unroll=2)
 
     def forward(n, _):
         j = plane - 1 - n
@@ -306,10 +297,15 @@
             device_id=plane_id(target), device_id_type=MESH,
         )
 
-    def gradients(j, i, seen):
+    def gradients(j, i, seen, split):
         where = pl.ds(i * block if isinstance(i, int) else pl.multiple_of(i * block, block), block)
-        p = jnp.exp2(s_all[j, i, :seen] - lse[i])
-        ds = (p * (dp_all[j, i, :seen] - delta[i])).astype(jnp.bfloat16)
+        if split is not None:
+            s = masked(dot(kv_all[j, 0, :seen], q_cols[i]) * LOG2_SCALE, split)
+            dp = dot(kv_all[j, 1, :seen], g_cols[i])
+        else:
+            s, dp = s_all[j, i], dp_all[j, i]
+        p = jnp.exp2(s - lse[i])
+        ds = (p * (dp - delta[i])).astype(jnp.bfloat16)
         p_all[:seen, where] = p.astype(jnp.bfloat16)
         ds_all[:seen, where] = ds
         if seen < chunk:
@@ -322,28 +318,30 @@
         k_cols[...] = kv_all[j, 0].T
 
         def one(i, _):
-            gradients(j, i, chunk)
+            gradients(j, i, chunk, None)
             return 0
 
         def triangle(h, _):
             for split in range(splits):
-                gradients(j, h * splits + split, (split + 1) * block)
+                gradients(j, h * splits + split, (split + 1) * block, split)
             return 0
 
         if diagonal:
             lax.fori_loop(0, group, triangle, 0, unroll=2)
         else:
             lax.fori_loop(0, jobs, one, 0, unroll=4)
-        for half, weights, lines in ((1, p_all, g_rows), (0, ds_all, q_rows)):
-            pair[j, half] = dot(weights[...], lines[...])
-            if not diagonal:
-                @pl.when(top_plane)
-                def _():
-                    part_out[j, half] = pair[j, half].astype(jnp.bfloat16)
-                    part_copy(j, half, plane - 1).start()
+        pair[j, 1] = dot(p_all[...], g_rows[...])
+        pair[j, 0] = dot(ds_all[...], q_rows[...])
 
     def earlier(j, _):
         backward(j, False)
+
+        @pl.when(top_plane)
+        def _():
+            for half in (1, 0):
+                part_out[j, half] = pair[j, half].astype(jnp.bfloat16)
+                part_copy(j, half, plane - 1).start()
+
         return 0
 
     lax.fori_loop(0, plane, earlier, 0)
@@ -477,8 +475,8 @@
             pltpu.VMEM((jobs, HEAD_WIDTH, block), f32),
             pltpu.VMEM((chunk, jobs * block), bf16),
             pltpu.VMEM((chunk, jobs * block), bf16),
-            pltpu.VMEM((planes, jobs, chunk, block), f32),
-            pltpu.VMEM((planes, jobs, chunk, block), f32),
+            pltpu.VMEM((max(planes - 1, 1), jobs, chunk, block), f32),
+            pltpu.VMEM((max(planes - 1, 1), jobs, chunk, block), f32),
             pltpu.VMEM((planes, 2, chunk, HEAD_WIDTH), f32),
             pltpu.VMEM((planes, 2, chunk, HEAD_WIDTH), bf16),
             pltpu.VMEM((planes, 2, chunk, HEAD_WIDTH), bf16),

time: 64.2 us -> 62.1 us (0.967)
  the two profiles are of different devices: /device:TPU:29 before, /device:TPU:0 now
where the time goes in v9:
time: 62.1 us; the launch traced here: 62 us
  Pallas kernels  61.3 us (99%)
  between operations  0.64 us (1%)
    pallas_call x1, Pallas kernels, shards(): pl.pallas_call(functools.partial(kernel, (tp, inner, planes, tok, group,...  59.2 us
    pallas_call x1, Pallas kernels, shards(): pl.pallas_call(hand_over, out_shape=tuple((jax.ShapeDtypeStruct(a.shape,...  2.16 us

profile of v9, /device:TPU:0, one launch (start us, length us, event | category | flops | bytes accessed | tf_op | source)
XLA Modules:
  0.0 62.0 jit_solution(4316622386607620014)
XLA Ops:
  0.6 59.2 %shard_map.75 = (bf16[64,4096]{1,0:T(8,128)(2,1)}, bf16[64,4096]{1,0:T(8,128)(2,1)}, bf16[64,1024]{1,0:T(8,128)(2,1)}, bf16[64,1024]{1,0:T(8,128)(2,1)}) custom-call(bf16[64,4096]{1,0:T(8,128)(2,1)} %query.1, bf16[64,1024]{1,0:T(8,128)(2,1)} %keys.1, bf16[64,1024]{1,0:T(8,128)(2,1)} %values.1, bf16[64,4096]{1,0:T(8,128)(2,1)} %grads.1), custom_call_target="tpu_custom_call" | custom-call | tf_op jit(solution)/shard_map/pallas_call | solution.py:449
  59.8 2.2 %shard_map.76 = (bf16[64,4096]{1,0:T(8,128)(2,1)}, bf16[64,4096]{1,0:T(8,128)(2,1)}, bf16[64,1024]{1,0:T(8,128)(2,1)}, bf16[64,1024]{1,0:T(8,128)(2,1)}) custom-call(bf16[64,4096]{1,0:T(8,128)(2,1)} %get-tuple-element.8.refs_0_, bf16[64,4096]{1,0:T(8,128)(2,1)} %get-tuple-element.9.refs_1_, bf16[64,1024]{1,0:T(8,128)(2,1)} %get-tuple-element.10.refs_2_, ...), custom_call_target="tpu_custom_call" | custom-call | tf_op jit(solution)/shard_map/pallas_call | solution.py:498
